TPU v7x, 512 devices: a whole 4x4x16 slice. The times are simulated.
512 devices in a mesh: grid: 256 (over z_lo, y, x, core), head: 2 (over z_hi).
Axes of the slice: x: 4, y: 4, z: 16 (z_hi: 2, z_lo: 8; z = z_hi * 8 + z_lo), core: 2. Of those that a mesh axis runs over, the one named last changes fastest.
Arguments:
- node_query: bfloat16 [8192, 1024], P('grid', 'head'), may hold values from -6 to 6
- node_key: bfloat16 [8192, 1024], P('grid', 'head'), may hold values from -6 to 6
- node_value: bfloat16 [8192, 1024], P('grid', 'head'), may hold values from -6 to 6
- out_grad: bfloat16 [8192, 1024], P('grid', 'head'), may hold values from -6 to 6
- tile_mask: int32 [256, 4, 4], P('grid'), may hold values from 0 to 1, as said below
- tile_type: int32 [256, 4, 4], P('grid'), may hold values from 0 to 15
- edge_table: float32 [16, 128], replicated, may hold values from -6 to 6
- edge_proj: float32 [128, 16], replicated, may hold values from -0.5 to 0.5
Outputs:
- attended: bfloat16 [8192, 1024], P('grid', 'head')
- query_grad: float32 [8192, 1024], P('grid', 'head')
- key_grad: float32 [8192, 1024], P('grid', 'head')
- value_grad: float32 [8192, 1024], P('grid', 'head')
- table_grad: float32 [16, 128], replicated
- proj_grad: float32 [128, 16], replicated
Inputs may be any that keep to these rules, and one draw needn't show every extreme that they name: `tile_mask`: tile (a, a) of block r * (17) is 1 for every a and r.
All inputs are finite; a program needn't handle non-finite values.
Results may differ from a plain program's by a relative error of at most 0.015.
Values may be sent and summed in bfloat16 or wider, within the bound.
A program may use at most 64 MiB of HBM per device.

v0:
```python
import math

import jax
import jax.numpy as jnp
from jax import lax
from jax.sharding import PartitionSpec as P

HEAD_DIM = 64
TILE = 128


neg_fill = -1e30
highest = lax.Precision.HIGHEST


def shortened(x):
    return jax.tree.map(lambda a: a.astype(jnp.bfloat16) if a.dtype == jnp.float32 else a, x)


def partner(block, axis, apart):
    count = lax.axis_size(axis)
    route = []
    for low in range(count):
        high = low | 1 << apart
        if high != low and high < count:
            route += [(low, high), (high, low)]
    return lax.ppermute(block, axis, route)


def levels_count():
    return (lax.axis_size("grid").bit_length() - 1) // 2


def index_bit(position):
    return jnp.right_shift(lax.axis_index("grid"), position) & 1


def select_by(condition, former, latter):
    return jax.tree.map(
        lambda first_leaf, second_leaf: jnp.where(condition, first_leaf, second_leaf),
        former,
        latter,
    )


def stack_rows(own_rows, far_rows, high_side):
    return tuple(
        (
            jnp.where(
                high_side,
                jnp.concatenate([far_piece, own_piece], 0),
                jnp.concatenate([own_piece, far_piece], 0),
            )
            for own_piece, far_piece in zip(own_rows, far_rows)
        )
    )


def add_members(former, latter, high_side):
    return tuple((first_part + second_part for first_part, second_part in zip(former, latter)))


def merge_softmax(former, latter, high_side):
    top_former, sum_former, acc_former = former
    top_latter, sum_latter, acc_latter = latter
    row_top = jnp.maximum(top_former, top_latter)
    scale_former = jnp.exp(top_former - row_top)
    scale_latter = jnp.exp(top_latter - row_top)
    row_count, head_count = row_top.shape
    weighted = acc_former.reshape(row_count, head_count, -1) * scale_former[:, :, None]
    weighted = weighted + acc_latter.reshape(row_count, head_count, -1) * scale_latter[:, :, None]
    return (
        row_top,
        sum_former * scale_former + sum_latter * scale_latter,
        weighted.reshape(row_count, -1),
    )


def collect_group(members, offset):
    for bit_level in range(levels_count()):
        arrived = jax.tree.map(
            lambda part, own: part.astype(own.dtype),
            partner(shortened(members), "grid", offset + bit_level),
            members,
        )
        members = stack_rows(members, arrived, index_bit(offset + bit_level) == 1)
    return members


def exchange_group(members, offset, combine, halving):
    levels = levels_count()
    bit_order = list(reversed(range(levels))) if halving else list(range(levels))
    for bit_level in bit_order:
        high_side = index_bit(offset + bit_level) == 1
        if halving:
            half_rows = members[0].shape[0] // 2
            low_half = tuple((member[:half_rows] for member in members))
            high_half = tuple((member[half_rows:] for member in members))
            outgoing = select_by(high_side, low_half, high_half)
            kept_half = select_by(high_side, high_half, low_half)
        else:
            outgoing = members
            kept_half = members
        arrived = partner(outgoing, "grid", offset + bit_level)
        members = combine(kept_half, arrived, high_side)
    return members


def route_bits(bit_level, levels):
    return (bit_level, bit_level + levels)


def mirror(members):
    levels = levels_count()
    for bit_level in range(levels):
        carried = members
        for step_bit in route_bits(bit_level, levels):
            carried = jax.tree.map(
                lambda part, own: part.astype(own.dtype),
                partner(shortened(carried), "grid", step_bit),
                carried,
            )
        differ = index_bit(bit_level) != index_bit(bit_level + levels)
        members = select_by(differ, carried, members)
    return members


def mirror_back(members):
    levels = levels_count()
    for bit_level in range(levels):
        carried = members
        for step_bit in route_bits(bit_level, levels):
            carried = partner(carried, "grid", step_bit)
        differ = index_bit(bit_level) != index_bit(bit_level + levels)
        members = select_by(differ, carried, members)
    return members


def per_device(
    node_query, node_key, node_value, out_grad, tile_mask, tile_type, edge_table, edge_proj
):
    levels = levels_count()
    piece_rows = node_query.shape[0]
    feature_width = node_query.shape[1]
    local_heads = feature_width // HEAD_DIM
    tile_count = tile_mask.shape[-1]
    group_rows = tile_count * TILE
    score_scale = 1.0 / math.sqrt(HEAD_DIM)
    (query_group,) = collect_group((node_query,), 0)
    mirrored = mirror(
        (node_key, node_value, tile_mask.astype(jnp.bfloat16), tile_type.astype(jnp.bfloat16))
    )
    key_group, value_group = collect_group((mirrored[0], mirrored[1]), levels)
    fwd_mask = tile_mask[0]
    fwd_type = tile_type[0]
    rev_mask = mirrored[2][0].astype(jnp.int32).T
    rev_type = mirrored[3][0].astype(jnp.int32).T
    type_ids = jnp.arange(edge_table.shape[0], dtype=jnp.int32)
    edge_hot = (fwd_type[:, :, None] == type_ids).astype(jnp.float32) * fwd_mask[:, :, None].astype(
        jnp.float32
    )
    edge_hot = edge_hot + (rev_type[:, :, None] == type_ids).astype(jnp.float32) * rev_mask[
        :, :, None
    ].astype(jnp.float32)
    head_start = lax.axis_index("head") * local_heads
    type_bias = jnp.dot(edge_table, edge_proj, precision=highest)
    local_bias = lax.dynamic_slice_in_dim(type_bias, head_start, local_heads, 1)
    tile_bias = jnp.einsum("abt,th->hab", edge_hot, local_bias, precision=highest)
    allowed = jnp.repeat(jnp.repeat(fwd_mask + rev_mask > 0, TILE, axis=0), TILE, axis=1)

    def split_heads(matrix):
        return matrix.reshape(matrix.shape[0], local_heads, HEAD_DIM).transpose(1, 0, 2)

    def join_heads(stacked):
        return stacked.transpose(1, 0, 2).reshape(stacked.shape[1], -1)

    def score_block(query_head, key_head, bias_head):
        scores = jnp.dot(query_head, key_head.T, preferred_element_type=jnp.float32) * score_scale
        scores = scores + jnp.repeat(jnp.repeat(bias_head, TILE, axis=0), TILE, axis=1)
        return jnp.where(allowed, scores, neg_fill)

    def forward_head(inputs):
        query_head, key_head, value_head, bias_head = inputs
        scores = score_block(query_head, key_head, bias_head)
        row_top = jnp.max(scores, axis=1)
        exps = jnp.where(allowed, jnp.exp(scores - row_top[:, None]), 0.0)
        weighted = jnp.dot(
            exps.astype(jnp.bfloat16), value_head, preferred_element_type=jnp.float32
        )
        return (row_top, jnp.sum(exps, axis=1), weighted)

    query_heads = split_heads(query_group)
    key_heads = split_heads(key_group)
    value_heads = split_heads(value_group)
    row_top, weight_sum, weighted = lax.map(
        forward_head, (query_heads, key_heads, value_heads, tile_bias)
    )
    softmax_state = (row_top.T, weight_sum.T, join_heads(weighted))
    top_group, sum_group, acc_group = exchange_group(softmax_state, 0, merge_softmax, False)
    unrounded_group = (
        acc_group.reshape(group_rows, local_heads, HEAD_DIM) / sum_group[:, :, None]
    ).reshape(group_rows, feature_width)
    row_start = lax.axis_index("grid") % (1 << levels) * piece_rows
    unrounded = lax.dynamic_slice_in_dim(unrounded_group, row_start, piece_rows, 0)
    (grad_group,) = collect_group((out_grad,), 0)
    logsum_group = top_group + jnp.log(sum_group)
    delta_group = jnp.sum(
        (grad_group.astype(jnp.float32) * unrounded_group).reshape(
            group_rows, local_heads, HEAD_DIM
        ),
        axis=2,
    )
    attended = unrounded.astype(jnp.bfloat16)

    def backward_head(inputs):
        query_head, key_head, value_head, grad_head, bias_head, logsum_head, delta_head = inputs
        scores = score_block(query_head, key_head, bias_head)
        probs = jnp.where(allowed, jnp.exp(scores - logsum_head[:, None]), 0.0)
        prob_grad = jnp.dot(grad_head, value_head.T, preferred_element_type=jnp.float32)
        score_grad = probs * (prob_grad - delta_head[:, None])
        probs_low = probs.astype(jnp.bfloat16)
        score_low = score_grad.astype(jnp.bfloat16)
        value_part = jnp.dot(probs_low.T, grad_head, preferred_element_type=jnp.float32)
        query_part = jnp.dot(score_low, key_head, preferred_element_type=jnp.float32) * score_scale
        key_part = (
            jnp.dot(score_low.T, query_head, preferred_element_type=jnp.float32) * score_scale
        )
        tile_sums = score_grad.reshape(tile_count, TILE, tile_count, TILE).sum(axis=(1, 3))
        return (query_part, key_part, value_part, tile_sums)

    query_part, key_part, value_part, tile_sums = lax.map(
        backward_head,
        (
            query_heads,
            key_heads,
            value_heads,
            split_heads(grad_group),
            tile_bias,
            logsum_group.T,
            delta_group.T,
        ),
    )
    (query_piece,) = exchange_group((join_heads(query_part),), 0, add_members, True)
    key_piece, value_piece = exchange_group(
        (join_heads(key_part), join_heads(value_part)), levels, add_members, True
    )
    key_grad, value_grad = mirror_back((key_piece, value_piece))
    local_grad = jnp.einsum("hab,abt->th", tile_sums, edge_hot, precision=highest)
    placed = lax.dynamic_update_slice_in_dim(
        jnp.zeros((edge_table.shape[0], edge_proj.shape[1]), jnp.float32), local_grad, head_start, 1
    )
    type_grad = lax.psum(placed, ("grid", "head"))
    table_grad = jnp.dot(type_grad, edge_proj.T, precision=highest)
    proj_grad = jnp.dot(edge_table.T, type_grad, precision=highest)
    return (attended, query_piece, key_grad, value_grad, table_grad, proj_grad)


def solution(mesh):
    return jax.shard_map(
        per_device,
        mesh=mesh,
        in_specs=(
            P("grid", "head"),
            P("grid", "head"),
            P("grid", "head"),
            P("grid", "head"),
            P("grid", None, None),
            P("grid", None, None),
            P(),
            P(),
        ),
        out_specs=(
            P("grid", "head"),
            P("grid", "head"),
            P("grid", "head"),
            P("grid", "head"),
            P(),
            P(),
        ),
        check_vma=False,
    )
```

profile of v0, /device:TPU:1, one launch (start us, length us, event | category | flops | bytes accessed | tf_op | source)
XLA Modules:
  0.0 766.6 jit_solution(1504299211143318140)
XLA Ops:
  1.6 8.9 %collective-permute-start = (bf16[32,512]{0,1:T(8,128)(2,1)S(1)}, bf16[32,512]{0,1:T(8,128)(2,1)S(1)}, u32[]{:S(2)}, u32[]{:S(2)}) collective-permute-start(bf16[32,512]{0,1:T(8,128)(2,1)S(1)} %copy.50), channel_id=1, source_target_pairs={{0,2},{2,0},{4,6},{6,4},{8,10},{10,8},{12,14},{14,12},{16,18},{18,... | collective-permute-start | bytes 98312 | tf_op jit(solution)/shard_map/ppermute | solution.py:27
  22.3 4.9 collective-permute-start.17
  39.9 4.9 collective-permute-start.20
  56.3 7.3 collective-permute-start.31
  65.7 6.2 collective-permute-done.23
  125.6 7.3 collective-permute-start.39
  132.9 7.7 %collective-permute-done.11 = bf16[32,512]{0,1:T(8,128)(2,1)S(1)} collective-permute-done((bf16[32,512]{0,1:T(8,128)(2,1)S(1)}, bf16[32,512]{0,1:T(8,128)(2,1)S(1)}, u32[]{:S(2)}, u32[]{:S(2)}) %collective-permute-start.11) | collective-permute-done | bytes 32800 | tf_op jit(solution)/shard_map/ppermute | solution.py:27
  163.0 4.9 collective-permute-start.15
  173.2 12.1 %collective-permute-done.15 = bf16[256,512]{0,1:T(8,128)(2,1)S(1)} collective-permute-done((bf16[256,512]{0,1:T(8,128)(2,1)S(1)}, bf16[256,512]{0,1:T(8,128)(2,1)S(1)}, u32[]{:S(2)}, u32[]{:S(2)}) %collective-permute-start.15) | collective-permute-done | bytes 262176 | tf_op jit(solution)/shard_map/ppermute | solution.py:27
  186.8 26.1 %collective-permute-done.43 = bf16[256,512]{0,1:T(8,128)(2,1)S(1)} collective-permute-done((bf16[256,512]{0,1:T(8,128)(2,1)S(1)}, bf16[256,512]{0,1:T(8,128)(2,1)S(1)}, u32[]{:S(2)}, u32[]{:S(2)}) %collective-permute-start.43) | collective-permute-done | bytes 262176 | tf_op jit(solution)/shard_map/ppermute | solution.py:27
  215.4 29.6 %while.32 = (s32[]{:T(128)}, f32[8,512]{1,0:T(8,128)S(1)}, f32[8,512]{1,0:T(8,128)S(1)}, f32[8,512,64]{1,2,0:T(8,128)}, bf16[8,512,64]{2,1,0:T(8,128)(2,1)S(1)},...) while((s32[]{:T(128)}, f32[8,512]{1,0:T(8,128)S(1)}, ...), condition=%wide.region_3.4_spmd.clone, body=%wide.region_0.3_spmd.clone.sunk | while | flops 69204992 | bytes 5820865 | solution.py:195
  245.0 5.7 collective-permute-start.45
  264.9 19.0 %collective-permute-done.53 = f32[512,8]{0,1:T(8,128)S(1)} collective-permute-done((f32[512,8]{0,1:T(8,128)S(1)}, f32[512,8]{0,1:T(8,128)S(1)}, u32[]{:S(2)}, u32[]{:S(2)}) %collective-permute-start.53) | collective-permute-done | bytes 16416 | tf_op jit(solution)/shard_map/ppermute | solution.py:27
  300.4 11.4 %collective-permute-done.54 = f32[512,8]{0,1:T(8,128)S(1)} collective-permute-done((f32[512,8]{0,1:T(8,128)S(1)}, f32[512,8]{0,1:T(8,128)S(1)}, u32[]{:S(2)}, u32[]{:S(2)}) %collective-permute-start.54) | collective-permute-done | bytes 16416 | tf_op jit(solution)/shard_map/ppermute | solution.py:27
  335.9 7.4 collective-permute-done.59
  349.0 81.1 %while.33 = (s32[]{:T(128)}, f32[8,512,64]{1,2,0:T(8,128)}, f32[8,512,64]{1,2,0:T(8,128)}, f32[8,512,64]{1,2,0:T(8,128)}, f32[8,4,4]{2,0,1:T(8,128)S(1)}, /*inde...) while((s32[]{:T(128)}, f32[8,512,64]{1,2,0:T(8,128)}, ...), condition=%wide.region_7.8_spmd.clone, body=%wide.region_5.7_spmd.clone.sunk | while | flops 170721264 | bytes 13274669 | solution.py:231
  437.4 113.8 %psum.7 = f32[16,16]{0,1:T(8,128)S(1)} all-reduce(f32[16,16]{0,1:T(8,128)S(1)} %fusion.50), channel_id=1, replica_groups=mesh['grid'=256,'head'=2] {'grid','head'}, use_global_device_ids=true, to_apply=%region_8.9 | all-reduce | flops 256 | bytes 2048 | tf_op jit(solution)/shard_map/psum | solution.py:252
  556.6 5.4 collective-permute-start.76
  569.5 40.6 %collective-permute-done.76 = f32[256,512]{0,1:T(8,128)S(1)} collective-permute-done((f32[256,512]{0,1:T(8,128)}, f32[256,512]{0,1:T(8,128)S(1)}, u32[]{:S(2)}, u32[]{:S(2)}) %collective-permute-start.76) | collective-permute-done | bytes 524320 | tf_op jit(solution)/shard_map/ppermute | solution.py:27
  614.3 9.9 %collective-permute-done.77 = f32[128,512]{0,1:T(8,128)S(1)} collective-permute-done((f32[128,512]{0,1:T(8,128)S(1)}, f32[128,512]{0,1:T(8,128)S(1)}, u32[]{:S(2)}, u32[]{:S(2)}) %collective-permute-start.77) | collective-permute-done | bytes 262176 | tf_op jit(solution)/shard_map/ppermute | solution.py:27
  688.0 5.2 collective-permute-start.63
  697.5 9.0 %collective-permute-done.73 = f32[32,512]{0,1:T(8,128)S(1)} collective-permute-done((f32[32,512]{0,1:T(8,128)S(1)}, f32[32,512]{0,1:T(8,128)S(1)}, u32[]{:S(2)}, u32[]{:S(2)}) %collective-permute-start.73) | collective-permute-done | bytes 65568 | tf_op jit(solution)/shard_map/ppermute | solution.py:27
  724.8 35.4 %collective-permute-done.75 = f32[32,512]{0,1:T(8,128)S(1)} collective-permute-done((f32[32,512]{0,1:T(8,128)S(1)}, f32[32,512]{0,1:T(8,128)S(1)}, u32[]{:S(2)}, u32[]{:S(2)}) %collective-permute-start.75) | collective-permute-done | bytes 65568 | tf_op jit(solution)/shard_map/ppermute | solution.py:27
  761.0 4.8 collective-permute-done.87
  (483 shorter events, 405.5 us)
Async XLA Ops:
  1.6 70.9 %collective-permute-start = (bf16[32,512]{0,1:T(8,128)(2,1)S(1)}, bf16[32,512]{0,1:T(8,128)(2,1)S(1)}, u32[]{:S(2)}, u32[]{:S(2)}) collective-permute-start(bf16[32,512]{0,1:T(8,128)(2,1)S(1)} %copy.50), channel_id=1, source_target_pairs={{0,2},{2,0},{4,6},{6,4},{8,10},{10,8},{12,14},{14,12},{16,18},{18,... | collective-permute-start | bytes 98312 | tf_op jit(solution)/shard_map/ppermute | solution.py:27
  10.6 63.9 %collective-permute-start.4 = (bf16[32,512]{0,1:T(8,128)(2,1)S(1)}, bf16[32,512]{0,1:T(8,128)(2,1)S(1)}, u32[]{:S(2)}, u32[]{:S(2)}) collective-permute-start(bf16[32,512]{0,1:T(8,128)(2,1)S(1)} %copy.61), channel_id=1, source_target_pairs={{0,2},{2,0},{4,6},{6,4},{8,10},{10,8},{12,14},{14,12},{16,18},{18,... | collective-permute-start | bytes 98312 | tf_op jit(solution)/shard_map/ppermute | solution.py:27
  17.1 61.5 %collective-permute-start.32 = (bf16[32,512]{0,1:T(8,128)(2,1)S(1)}, bf16[32,512]{0,1:T(8,128)(2,1)S(1)}, u32[]{:S(2)}, u32[]{:S(2)}) collective-permute-start(bf16[32,512]{0,1:T(8,128)(2,1)S(1)} %copy.65), channel_id=1, source_target_pairs={{0,2},{2,0},{4,6},{6,4},{8,10},{10,8},{12,14},{14,12},{16,18},{18,... | collective-permute-start | bytes 98312 | tf_op jit(solution)/shard_map/ppermute | solution.py:27
  72.6 19.6 %collective-permute-start.1 = (bf16[64,512]{0,1:T(8,128)(2,1)S(1)}, bf16[64,512]{0,1:T(8,128)(2,1)S(1)}, u32[]{:S(2)}, u32[]{:S(2)}) collective-permute-start(bf16[64,512]{0,1:T(8,128)(2,1)S(1)} %maximum_select_fusion.12), channel_id=1, source_target_pairs={{0,4},{4,0},{2,6},{6,2},{8,12},{12,8},{10,14},{14,10},{16,20},{20,... | collective-permute-start | bytes 196616 | tf_op jit(solution)/shard_map/ppermute | solution.py:27
  92.4 27.7 %collective-permute-start.2 = (bf16[128,512]{0,1:T(8,128)(2,1)S(1)}, bf16[128,512]{0,1:T(8,128)(2,1)S(1)}, u32[]{:S(2)}, u32[]{:S(2)}) collective-permute-start(bf16[128,512]{0,1:T(8,128)(2,1)S(1)} %maximum_select_fusion.13), channel_id=1, source_target_pairs={{0,8},{8,0},{2,10},{10,2},{4,12},{12,4},{6,14},{14,6},{16,24},{24,... | collective-permute-start | bytes 393224 | tf_op jit(solution)/shard_map/ppermute | solution.py:27
  120.2 52.3 %collective-permute-start.3 = (bf16[256,512]{0,1:T(8,128)(2,1)S(1)}, bf16[256,512]{0,1:T(8,128)(2,1)S(1)}, u32[]{:S(2)}, u32[]{:S(2)}) collective-permute-start(bf16[256,512]{0,1:T(8,128)(2,1)S(1)} %maximum_select_fusion.4), channel_id=1, source_target_pairs={{0,16},{16,0},{2,18},{18,2},{4,20},{20,4},{6,22},{22,6},{8,24},{24... | collective-permute-start | bytes 786440 | tf_op jit(solution)/shard_map/ppermute | solution.py:27
  163.0 22.3 %collective-permute-start.15 = (bf16[256,512]{0,1:T(8,128)(2,1)S(1)}, bf16[256,512]{0,1:T(8,128)(2,1)S(1)}, u32[]{:S(2)}, u32[]{:S(2)}) collective-permute-start(bf16[256,512]{0,1:T(8,128)(2,1)S(1)} %maximum_select_fusion.6), channel_id=1, source_target_pairs={{0,256},{256,0},{2,258},{258,2},{4,260},{260,4},{6,262},{262,6},{8... | collective-permute-start | bytes 786440 | tf_op jit(solution)/shard_map/ppermute | solution.py:27
  168.0 44.8 %collective-permute-start.43 = (bf16[256,512]{0,1:T(8,128)(2,1)S(1)}, bf16[256,512]{0,1:T(8,128)(2,1)S(1)}, u32[]{:S(2)}, u32[]{:S(2)}) collective-permute-start(bf16[256,512]{0,1:T(8,128)(2,1)S(1)} %maximum_select_fusion.8), channel_id=1, source_target_pairs={{0,256},{256,0},{2,258},{258,2},{4,260},{260,4},{6,262},{262,6},{8... | collective-permute-start | bytes 786440 | tf_op jit(solution)/shard_map/ppermute | solution.py:27
  257.3 27.0 %collective-permute-start.47 = (f32[512,512]{0,1:T(8,128)S(1)}, f32[512,512]{0,1:T(8,128)S(1)}, u32[]{:S(2)}, u32[]{:S(2)}) collective-permute-start(f32[512,512]{0,1:T(8,128)S(1)} %bitcast.249), channel_id=1, source_target_pairs={{0,4},{4,0},{2,6},{6,2},{8,12},{12,8},{10,14},{14,10},{16,20},{20,... | collective-permute-start | bytes 3145736 | tf_op jit(solution)/shard_map/ppermute | solution.py:27
  259.6 24.3 %collective-permute-start.53 = (f32[512,8]{0,1:T(8,128)S(1)}, f32[512,8]{0,1:T(8,128)S(1)}, u32[]{:S(2)}, u32[]{:S(2)}) collective-permute-start(f32[512,8]{0,1:T(8,128)S(1)} %get-tuple-element.290), channel_id=1, source_target_pairs={{0,4},{4,0},{2,6},{6,2},{8,12},{12,8},{10,14},{14,10},{16,20},{20,... | collective-permute-start | bytes 49160 | tf_op jit(solution)/shard_map/ppermute | solution.py:27
  262.6 21.7 %collective-permute-start.46 = (f32[512,8]{0,1:T(8,128)S(1)}, f32[512,8]{0,1:T(8,128)S(1)}, u32[]{:S(2)}, u32[]{:S(2)}) collective-permute-start(f32[512,8]{0,1:T(8,128)S(1)} %get-tuple-element.293), channel_id=1, source_target_pairs={{0,4},{4,0},{2,6},{6,2},{8,12},{12,8},{10,14},{14,10},{16,20},{20,... | collective-permute-start | bytes 49160 | tf_op jit(solution)/shard_map/ppermute | solution.py:27
  284.6 27.6 %collective-permute-start.49 = (f32[512,512]{0,1:T(8,128)S(1)}, f32[512,512]{0,1:T(8,128)S(1)}, u32[]{:S(2)}, u32[]{:S(2)}) collective-permute-start(f32[512,512]{0,1:T(8,128)S(1)} %bitcast.248), channel_id=1, source_target_pairs={{0,8},{8,0},{2,10},{10,2},{4,12},{12,4},{6,14},{14,6},{16,24},{24,... | collective-permute-start | bytes 3145736 | tf_op jit(solution)/shard_map/ppermute | solution.py:27
  291.0 20.8 %collective-permute-start.54 = (f32[512,8]{0,1:T(8,128)S(1)}, f32[512,8]{0,1:T(8,128)S(1)}, u32[]{:S(2)}, u32[]{:S(2)}) collective-permute-start(f32[512,8]{0,1:T(8,128)S(1)} %get-tuple-element.286), channel_id=1, source_target_pairs={{0,8},{8,0},{2,10},{10,2},{4,12},{12,4},{6,14},{14,6},{16,24},{24,... | collective-permute-start | bytes 49160 | tf_op jit(solution)/shard_map/ppermute | solution.py:27
  314.7 29.6 %collective-permute-start.51 = (f32[512,512]{0,1:T(8,128)S(1)}, f32[512,512]{0,1:T(8,128)S(1)}, u32[]{:S(2)}, u32[]{:S(2)}) collective-permute-start(f32[512,512]{0,1:T(8,128)S(1)} %bitcast.250), channel_id=1, source_target_pairs={{0,16},{16,0},{2,18},{18,2},{4,20},{20,4},{6,22},{22,6},{8,24},{24... | collective-permute-start | bytes 3145736 | tf_op jit(solution)/shard_map/ppermute | solution.py:27
  431.3 130.6 %collective-permute-start.60 = (f32[256,512]{0,1:T(8,128)S(1)}, f32[256,512]{0,1:T(8,128)}, u32[]{:S(2)}, u32[]{:S(2)}) collective-permute-start(f32[256,512]{0,1:T(8,128)S(1)} %bitcast.266), channel_id=1, source_target_pairs={{0,16},{16,0},{2,18},{18,2},{4,20},{20,4},{6,22},{22,6},{8,24},{24... | collective-permute-start | bytes 1572872 | tf_op jit(solution)/shard_map/ppermute | solution.py:27
  435.3 132.1 %collective-permute-start.64 = (f32[256,512]{0,1:T(8,128)S(1)}, f32[256,512]{0,1:T(8,128)S(1)}, u32[]{:S(2)}, u32[]{:S(2)}) collective-permute-start(f32[256,512]{0,1:T(8,128)S(1)} %bitcast.265), channel_id=1, source_target_pairs={{0,256},{256,0},{2,258},{258,2},{4,260},{260,4},{6,262},{262,6},{8... | collective-permute-start | bytes 1572872 | tf_op jit(solution)/shard_map/ppermute | solution.py:27
  556.6 53.5 %collective-permute-start.76 = (f32[256,512]{0,1:T(8,128)}, f32[256,512]{0,1:T(8,128)S(1)}, u32[]{:S(2)}, u32[]{:S(2)}) collective-permute-start(f32[256,512]{0,1:T(8,128)} %bitcast.267), channel_id=1, source_target_pairs={{0,256},{256,0},{2,258},{258,2},{4,260},{260,4},{6,262},{262,6},{8... | collective-permute-start | bytes 1572872 | tf_op jit(solution)/shard_map/ppermute | solution.py:27
  563.1 63.2 %collective-permute-start.61 = (f32[128,512]{0,1:T(8,128)S(1)}, f32[128,512]{0,1:T(8,128)S(1)}, u32[]{:S(2)}, u32[]{:S(2)}) collective-permute-start(f32[128,512]{0,1:T(8,128)S(1)} %slice_select_fusion.14), channel_id=1, source_target_pairs={{0,8},{8,0},{2,10},{10,2},{4,12},{12,4},{6,14},{14,6},{16,24},{24,... | collective-permute-start | bytes 786440 | tf_op jit(solution)/shard_map/ppermute | solution.py:27
  567.5 44.7 %collective-permute-start.65 = (f32[128,512]{0,1:T(8,128)S(1)}, f32[128,512]{0,1:T(8,128)S(1)}, u32[]{:S(2)}, u32[]{:S(2)}) collective-permute-start(f32[128,512]{0,1:T(8,128)S(1)} %slice_select_fusion.11), channel_id=1, source_target_pairs={{0,128},{128,0},{2,130},{130,2},{4,132},{132,4},{6,134},{134,6},{8... | collective-permute-start | bytes 786440 | tf_op jit(solution)/shard_map/ppermute | solution.py:27
  685.4 21.1 %collective-permute-start.73 = (f32[32,512]{0,1:T(8,128)S(1)}, f32[32,512]{0,1:T(8,128)S(1)}, u32[]{:S(2)}, u32[]{:S(2)}) collective-permute-start(f32[32,512]{0,1:T(8,128)S(1)} %collective-permute-done.72), channel_id=1, source_target_pairs={{0,128},{128,0},{2,130},{130,2},{4,132},{132,4},{6,134},{134,6},{8... | collective-permute-start | bytes 196616 | tf_op jit(solution)/shard_map/ppermute | solution.py:27
  688.0 30.4 %collective-permute-start.63 = (f32[32,512]{0,1:T(8,128)S(1)}, f32[32,512]{0,1:T(8,128)S(1)}, u32[]{:S(2)}, u32[]{:S(2)}) collective-permute-start(f32[32,512]{0,1:T(8,128)S(1)} %slice_select_fusion.12), channel_id=1, source_target_pairs={{0,2},{2,0},{4,6},{6,4},{8,10},{10,8},{12,14},{14,12},{16,18},{18,... | collective-permute-start | bytes 196616 | tf_op jit(solution)/shard_map/ppermute | solution.py:27
  693.3 18.9 %collective-permute-start.85 = (f32[32,512]{0,1:T(8,128)S(1)}, f32[32,512]{0,1:T(8,128)S(1)}, u32[]{:S(2)}, u32[]{:S(2)}) collective-permute-start(f32[32,512]{0,1:T(8,128)S(1)} %collective-permute-done.84), channel_id=1, source_target_pairs={{0,128},{128,0},{2,130},{130,2},{4,132},{132,4},{6,134},{134,6},{8... | collective-permute-start | bytes 196616 | tf_op jit(solution)/shard_map/ppermute | solution.py:27
  714.1 46.1 %collective-permute-start.75 = (f32[32,512]{0,1:T(8,128)S(1)}, f32[32,512]{0,1:T(8,128)S(1)}, u32[]{:S(2)}, u32[]{:S(2)}) collective-permute-start(f32[32,512]{0,1:T(8,128)S(1)} %collective-permute-done.74), channel_id=1, source_target_pairs={{0,256},{256,0},{2,258},{258,2},{4,260},{260,4},{6,262},{262,6},{8... | collective-permute-start | bytes 196616 | tf_op jit(solution)/shard_map/ppermute | solution.py:27
  721.3 44.5 %collective-permute-start.87 = (f32[32,512]{0,1:T(8,128)S(1)}, f32[32,512]{0,1:T(8,128)S(1)}, u32[]{:S(2)}, u32[]{:S(2)}) collective-permute-start(f32[32,512]{0,1:T(8,128)S(1)} %collective-permute-done.86), channel_id=1, source_target_pairs={{0,256},{256,0},{2,258},{258,2},{4,260},{260,4},{6,262},{262,6},{8... | collective-permute-start | bytes 196616 | tf_op jit(solution)/shard_map/ppermute | solution.py:27
  (77 other events, 664.2 us)
where the time goes:
time: 771 us; the launch traced here: 767 us
  starting transfers between devices  274 us (36%)
  waiting for transfers between devices  229 us (30%)
  blocking collectives  114 us (15%)
  matrix products  83.7 us (11%)
  local copies, waits for them, and re-layouts  40.4 us (5%)
  other arithmetic  22.8 us (3%)
    ppermute x88, starting transfers between devices, partner(): return lax.ppermute(block, axis, route)  274 us
    ppermute x88, waiting for transfers between devices, partner(): return lax.ppermute(block, axis, route)  229 us
    psum x1, blocking collectives, per_device(): type_grad = lax.psum(placed, ('grid', 'head'))  114 us
    dot_general x16, matrix products, score_block(): jnp.dot(query_head, key_head.T, preferred_element_type=jnp.float32)  21.2 us
  transfers between devices with their start and end apart: 88, of which 38 were waited for; matrix products, arithmetic and copies ran while one was open for 3% of the time, Pallas kernels for 0%

commit v1 on v0

v1 whole, which is shorter than its diff:
```python
import jax
import jax.numpy as jnp
from jax import lax
from jax.experimental import pallas as pl
from jax.experimental.pallas import tpu as pltpu
from jax.sharding import PartitionSpec as P

F32 = jnp.float32
BF16 = jnp.bfloat16
MESH = pl.DeviceIdType.MESH

NZ, NY, NX, NC = 8, 4, 4, 2
NXC = NX * NC
ROWS = 32
HD = 64
TILE_TYPES = 16
QN = NY * NZ * ROWS
KB = NZ * ROWS
MASKED = -1e30

(G_AQ, G_AK, G_MX, G_MY, G_MZ, G_QD, G_ST, G_O, G_DQ, G_RS, G_TX, G_TY, G_TZ, G_X1, G_X2, G_KV) = range(16)
N_SEMS = 16 + NXC

QCHUNK = 512


def dot_nt(a, b):
    return lax.dot_general(a, b, (((1,), (1,)), ((), ())), preferred_element_type=F32)


def dot_tn(a, b):
    return lax.dot_general(a, b, (((0,), (0,)), ((), ())), preferred_element_type=F32)


def dot_nn(a, b):
    return lax.dot_general(a, b, (((1,), (0,)), ((), ())), preferred_element_type=F32)


def split3(x):
    hi = x.astype(BF16)
    rest = x - hi.astype(F32)
    mid = rest.astype(BF16)
    low = (rest - mid.astype(F32)).astype(BF16)
    return hi, mid, low


def iota(shape, dim):
    return lax.broadcasted_iota(jnp.int32, shape, dim)


def kernel(
    q_ref, k_ref, v_ref, do_ref, mask_ref, type_ref, table_ref, proj_ref,
    att_ref, dq_ref, dk_ref, dv_ref, dtable_ref, dproj_ref,
    stq, stk, qd, kvb, q0, d0, qbias, konehot, expand,
    mx, my, tiles, fsel, gsel, projt, square,
    exps, dprob, tops, stat, out_t, dqt, tsum,
    osend, orecv, dsend, drecv, rsend, rrecv,
    tx, ty, tz, x1s, x1r, x2s, x2r,
    send, recv,
):
    g = lax.axis_index("grid")
    zh = lax.axis_index("head")
    core = g % 2
    x = (g // 2) % 4
    y = (g // 8) % 4
    z = g // 32
    xc = g % 8
    zf = zh * NZ + z

    def dev(z_, y_, xc_, zh_):
        return ((z_ * NY + y_) * NXC + xc_, zh_)

    def put(src, dst, group, where, slot=None):
        pltpu.make_async_remote_copy(
            src_ref=src, dst_ref=dst, send_sem=send.at[group],
            recv_sem=recv.at[group if slot is None else slot],
            device_id=where, device_id_type=MESH,
        ).start()

    def await_bytes(ref, sem):
        pltpu.make_async_copy(ref, ref, sem).wait()

    z_peers = [(z + d) % NZ for d in range(1, NZ)]
    y_peers = [(y + d) % NY for d in range(1, NY)]
    xc_peers = [(xc + d) % NXC for d in range(1, NXC)]
    zf_peers = [(zf + d) % (2 * NZ) for d in range(1, 2 * NZ)]

    barrier = pltpu.get_barrier_semaphore()
    for p in xc_peers:
        pl.semaphore_signal(barrier, inc=1, device_id=dev(z, y, p, zh), device_id_type=MESH)
    for p in y_peers:
        pl.semaphore_signal(barrier, inc=1, device_id=dev(z, p, xc, zh), device_id_type=MESH)
    for p in zf_peers:
        pl.semaphore_signal(barrier, inc=1, device_id=dev(p % NZ, y, xc, p // NZ), device_id_type=MESH)

    row_base = (y // 2) * 4
    lane_base = ((y % 2) * 8 + xc) * 4
    rows8 = iota((8, 128), 0)
    lanes8 = iota((8, 128), 1)
    code = jnp.zeros((8, 128), jnp.int32)
    for a in range(4):
        for b in range(4):
            value = mask_ref[0, a, b] * (type_ref[0, a, b] + 1)
            code = jnp.where((rows8 == row_base + a) & (lanes8 == lane_base + b), value, code)
    mx[xc] = code.astype(F32)

    for h in range(NZ):
        cols = slice(h * HD, (h + 1) * HD)
        scaled = (q_ref[:, cols].astype(F32) * 0.125).astype(BF16)
        stq[h] = jnp.concatenate([scaled, do_ref[:, cols]], axis=1)
        stk[h] = jnp.concatenate([k_ref[:, cols], v_ref[:, cols]], axis=1)

    pl.semaphore_wait(barrier, len(xc_peers) + len(y_peers) + len(zf_peers))

    own_rows = pl.ds(pl.multiple_of(z * ROWS, ROWS), ROWS)
    for p in xc_peers:
        put(mx.at[xc], mx.at[xc], G_MX, dev(z, y, p, zh))
    for p in z_peers:
        put(stk.at[p], kvb.at[xc, own_rows], G_AK, dev(p, y, xc, zh))
        put(stq.at[p], qd.at[y, own_rows], G_AQ, dev(p, y, xc, zh))
    kvb[xc, own_rows] = stk[z]
    qd[y, own_rows] = stq[z]

    square[...] = jnp.zeros((128, 128), F32)
    square[:, 0:16] = proj_ref[...]
    projt[...] = jnp.transpose(square[...])[0:16]
    kn = iota((KB, 128), 1)
    kt = iota((KB, 128), 0) // ROWS
    for par in range(2):
        konehot[par] = jnp.where((kn < 48) & (kn % 16 == 2 * kt + par), 1.0, 0.0).astype(BF16)
    qi = iota((QN, 128), 0)
    q_tile = 8 * ((qi % KB) // ROWS) + 2 * (qi // KB) + x // 2
    expand[...] = jnp.where(iota((QN, 128), 1) == q_tile, 1.0, 0.0).astype(BF16)
    stat[y] = jnp.where(iota((8, QN), 0) == 0, -3e38, 0.0)
    out_t[...] = jnp.zeros_like(out_t)
    dqt[...] = jnp.zeros_like(dqt)
    tsum[...] = jnp.zeros_like(tsum)

    await_bytes(mx.at[pl.ds(0, 7)], recv.at[G_MX])
    total = mx[0]
    for i in range(1, NXC):
        total = total + mx[i]
    my[y] = total
    for p in y_peers:
        put(my.at[y], my.at[y], G_MY, dev(z, p, xc, zh))
    await_bytes(my.at[pl.ds(0, 3)], recv.at[G_MY])
    tiles[z] = my[0] + my[1] + my[2] + my[3]
    for p in z_peers:
        put(tiles.at[z], tiles.at[z], G_MZ, dev(p, y, xc, zh))

    await_bytes(stk.at[pl.ds(0, 7)], recv.at[G_AK])
    for p in xc_peers:
        put(kvb.at[xc], kvb.at[xc], G_KV, dev(z, y, p, zh), slot=16 + xc)
    await_bytes(stq.at[pl.ds(0, 7)], recv.at[G_AQ])
    for p in y_peers:
        put(qd.at[y], qd.at[y], G_QD, dev(z, p, xc, zh))

    await_bytes(tiles.at[pl.ds(0, 7)], recv.at[G_MZ])
    fcode = tiles[...].reshape(64, 128)
    square[0:64] = fcode
    square[64:128] = jnp.zeros((64, 128), F32)
    gcode = jnp.transpose(square[...])[0:64]
    own_proj = projt[pl.ds(zf, 1), :]
    type_bias = jnp.sum(table_ref[...] * own_proj, axis=1, keepdims=True)
    type_bias = jnp.broadcast_to(type_bias, (TILE_TYPES, 128))
    bias = jnp.zeros((64, 128), F32)
    for t in range(TILE_TYPES):
        here = type_bias[t : t + 1, :]
        bias = bias + jnp.where(fcode == t + 1.0, here, 0.0) + jnp.where(gcode == t + 1.0, here, 0.0)
    bias = jnp.where(fcode + gcode > 0.0, bias, MASKED)
    sel_n = iota((128, 128), 1)
    sel_b = sel_n % 16
    column = iota((128, 128), 0) == 8 * (sel_b // 2) + 2 * y + sel_b % 2
    columns = jnp.zeros((64, 128), F32)
    for part, piece in enumerate(split3(bias)):
        pick = jnp.where(column & (sel_n // 16 == part), 1.0, 0.0).astype(BF16)
        columns = columns + dot_nn(piece, pick)
    columns = columns.astype(BF16)
    qbias[...] = dot_nn(expand[:, 0:64], columns).astype(BF16)
    kr = iota((16, 64), 0)
    pick_rows = jnp.where(iota((16, 64), 1) == 8 * (kr % 8) + 2 * y + kr // 8, 1.0, 0.0).astype(BF16)
    fsel[...] = dot_nn(pick_rows, gcode.astype(BF16))
    gsel[...] = dot_nn(pick_rows, fcode.astype(BF16))

    await_bytes(qd.at[pl.ds(0, 3)], recv.at[G_QD])
    low_lanes = jnp.where(iota((1, 128), 1) < HD, 1.0, 0.0)
    both = qd[...].reshape(QN, 128).astype(F32)
    q0[...] = (both * low_lanes).astype(BF16)
    d0[...] = (both * (1.0 - low_lanes)).astype(BF16)

    chunks = [slice(c * QCHUNK, (c + 1) * QCHUNK) for c in range(QN // QCHUNK)]

    def block_at(s):
        i = s // 2
        dx = i + (i // 2) * (5 - 2 * i)
        return ((x + dx) % NX) * 2 + (core + s) % 2

    def forward(s, carry):
        j = block_at(s)

        @pl.when(s > 0)
        def _():
            await_bytes(kvb.at[j], recv.at[16 + j])

        kv = kvb[j]
        wide = jnp.concatenate([kv, konehot[j // 4]], axis=1)
        for cs in chunks:
            scores = dot_nt(wide, jnp.concatenate([q0[cs], qbias[cs]], axis=1))
            dp = dot_nt(kv, d0[cs])
            dprob[j, :, cs] = dp
            old = stat[y, 0:1, cs]
            top = jnp.maximum(old, jnp.max(scores, axis=0, keepdims=True))
            e = jnp.exp(scores - top)
            shrink = jnp.exp(old - top)
            eb = e.astype(BF16)
            exps[j, :, cs] = eb
            stat[y, 0:1, cs] = top
            stat[y, 1:2, cs] = stat[y, 1:2, cs] * shrink + jnp.sum(e, axis=0, keepdims=True)
            stat[y, 2:3, cs] = stat[y, 2:3, cs] * shrink + jnp.sum(e * dp, axis=0, keepdims=True)
            tops[j, 0:1, cs] = top
            out_t[:, cs] = out_t[:, cs] * shrink + dot_tn(kv, eb)
        return carry

    lax.fori_loop(0, NXC, forward, 0)

    for p in y_peers:
        put(stat.at[y], stat.at[y], G_ST, dev(z, p, xc, zh))
    await_bytes(stat.at[pl.ds(0, 3)], recv.at[G_ST])
    top = stat[0, 0:1, :]
    for i in range(1, NY):
        top = jnp.maximum(top, stat[i, 0:1, :])
    weight_sum = jnp.zeros((1, QN), F32)
    delta = jnp.zeros((1, QN), F32)
    for i in range(NY):
        scale = jnp.exp(stat[i, 0:1, :] - top)
        weight_sum = weight_sum + stat[i, 1:2, :] * scale
        delta = delta + stat[i, 2:3, :] * scale
    delta = delta / weight_sum
    logsum = top + jnp.log(weight_sum)
    own_scale = jnp.exp(stat[y, 0:1, :] - top) / weight_sum
    for p in range(NY):
        cs = slice(p * KB, (p + 1) * KB)
        osend[p] = out_t[HD : 2 * HD, cs] * own_scale[:, cs]
    orecv[y] = osend[y]
    for p in y_peers:
        put(osend.at[p], orecv.at[y], G_O, dev(z, p, xc, zh))

    def backward(s, carry):
        j = block_at(NXC - 1 - s)
        kv = kvb[j]
        dkv = jnp.zeros((KB, 128), F32)
        for cs in chunks:
            sigma = jnp.exp(tops[j, 0:1, cs] - logsum[:, cs])
            p = exps[j, :, cs].astype(F32) * sigma
            ds = p * (dprob[j, :, cs] - delta[:, cs])
            pb = p.astype(BF16)
            dsb = ds.astype(BF16)
            dkv = dkv + dot_nn(pb, d0[cs]) + dot_nn(dsb, q0[cs])
            dqt[:, cs] = dqt[:, cs] + dot_tn(kv, dsb)
            tsum[j // 4, :, cs] = tsum[j // 4, :, cs] + jnp.sum(ds.reshape(NZ, ROWS, QCHUNK), axis=1)
        rsend[j] = dkv.astype(BF16)

        @pl.when(s < NXC - 1)
        def _():
            put(rsend.at[j], rrecv.at[xc], G_RS, dev(z, y, j, zh))

        return carry

    lax.fori_loop(0, NXC, backward, 0)
    rrecv[xc] = rsend[xc]

    for p in range(NY):
        dsend[p] = (dqt[0:HD, p * KB : (p + 1) * KB] * 0.125).astype(BF16)
    drecv[y] = dsend[y]
    for p in y_peers:
        put(dsend.at[p], drecv.at[y], G_DQ, dev(z, p, xc, zh))

    sums = jnp.zeros((16, 128), F32)
    for piece in split3(tsum[...].reshape(16, QN)):
        sums = sums + dot_nn(piece, expand[...])
    for t in range(TILE_TYPES):
        hits = jnp.where(fsel[...] == t + 1.0, sums, 0.0) + jnp.where(gsel[...] == t + 1.0, sums, 0.0)
        tx[xc, t : t + 1, :] = jnp.sum(hits, axis=0, keepdims=True)
    for p in xc_peers:
        put(tx.at[xc], tx.at[xc], G_TX, dev(z, y, p, zh))

    await_bytes(rrecv.at[pl.ds(0, 7)], recv.at[G_RS])
    total = rrecv[0].astype(F32)
    for i in range(1, NXC):
        total = total + rrecv[i].astype(F32)
    x2s[...] = total.astype(BF16).reshape(NZ, ROWS, 128)
    for p in z_peers:
        put(x2s.at[p], x2r.at[z], G_X2, dev(p, y, xc, zh))
    x2r[z] = x2s[z]

    await_bytes(orecv.at[pl.ds(0, 3)], recv.at[G_O])
    await_bytes(drecv.at[pl.ds(0, 3)], recv.at[G_DQ])
    att = orecv[0] + orecv[1] + orecv[2] + orecv[3]
    dq = drecv[0].astype(F32) + drecv[1].astype(F32) + drecv[2].astype(F32) + drecv[3].astype(F32)
    pair = jnp.transpose(jnp.concatenate([att, dq], axis=0))
    x1s[...] = pair.astype(BF16).reshape(NZ, ROWS, 128)
    for p in z_peers:
        put(x1s.at[p], x1r.at[z], G_X1, dev(p, y, xc, zh))
    x1r[z] = x1s[z]

    await_bytes(tx.at[pl.ds(0, 7)], recv.at[G_TX])
    total = tx[0]
    for i in range(1, NXC):
        total = total + tx[i]
    ty[y] = total
    for p in y_peers:
        put(ty.at[y], ty.at[y], G_TY, dev(z, p, xc, zh))
    await_bytes(ty.at[pl.ds(0, 3)], recv.at[G_TY])
    total = ty[0] + ty[1] + ty[2] + ty[3]
    tz[zf] = jnp.broadcast_to(jnp.sum(total, axis=1, keepdims=True), (TILE_TYPES, 128))
    for p in zf_peers:
        put(tz.at[zf], tz.at[zf], G_TZ, dev(p % NZ, y, xc, p // NZ))

    await_bytes(x2r.at[pl.ds(0, 7)], recv.at[G_X2])
    for h in range(NZ):
        cols = slice(h * HD, (h + 1) * HD)
        dk_ref[:, cols] = x2r[h][:, 0:HD].astype(F32)
        dv_ref[:, cols] = x2r[h][:, HD : 2 * HD].astype(F32)
    await_bytes(x1r.at[pl.ds(0, 7)], recv.at[G_X1])
    for h in range(NZ):
        cols = slice(h * HD, (h + 1) * HD)
        att_ref[:, cols] = x1r[h][:, 0:HD]
        dq_ref[:, cols] = x1r[h][:, HD : 2 * HD].astype(F32)

    await_bytes(tz.at[pl.ds(0, 15)], recv.at[G_TZ])
    dtable = jnp.zeros((TILE_TYPES, 128), F32)
    square[...] = jnp.zeros((128, 128), F32)
    for h in range(2 * NZ):
        dtable = dtable + tz[h] * projt[h : h + 1, :]
        square[h : h + 1, :] = jnp.sum(tz[h] * table_ref[...], axis=0, keepdims=True)
    dtable_ref[...] = dtable
    dproj_ref[...] = jnp.transpose(square[...])[:, 0:16]

    for ref, group in (
        (stk.at[pl.ds(0, 7)], G_AK), (stq.at[pl.ds(0, 7)], G_AQ), (mx.at[pl.ds(0, 7)], G_MX),
        (my.at[pl.ds(0, 3)], G_MY), (tiles.at[pl.ds(0, 7)], G_MZ), (qd.at[pl.ds(0, 3)], G_QD),
        (kvb.at[pl.ds(0, 7)], G_KV), (stat.at[pl.ds(0, 3)], G_ST), (osend.at[pl.ds(0, 3)], G_O),
        (dsend.at[pl.ds(0, 3)], G_DQ), (rsend.at[pl.ds(0, 7)], G_RS), (tx.at[pl.ds(0, 7)], G_TX),
        (ty.at[pl.ds(0, 3)], G_TY), (tz.at[pl.ds(0, 15)], G_TZ), (x1s.at[pl.ds(0, 7)], G_X1),
        (x2s.at[pl.ds(0, 7)], G_X2),
    ):
        await_bytes(ref, send.at[group])


def per_device(node_query, node_key, node_value, out_grad, tile_mask, tile_type, edge_table, edge_proj):
    vmem = pl.BlockSpec(memory_space=pltpu.VMEM)
    smem = pl.BlockSpec(memory_space=pltpu.SMEM)
    half = (ROWS, NZ * HD)
    return pl.pallas_call(
        kernel,
        out_shape=(
            jax.ShapeDtypeStruct(half, BF16),
            jax.ShapeDtypeStruct(half, F32),
            jax.ShapeDtypeStruct(half, F32),
            jax.ShapeDtypeStruct(half, F32),
            jax.ShapeDtypeStruct((TILE_TYPES, 128), F32),
            jax.ShapeDtypeStruct((128, TILE_TYPES), F32),
        ),
        in_specs=[vmem] * 4 + [smem] * 2 + [vmem] * 2,
        out_specs=(vmem,) * 6,
        scratch_shapes=[
            pltpu.VMEM((NZ, ROWS, 128), BF16),
            pltpu.VMEM((NZ, ROWS, 128), BF16),
            pltpu.VMEM((NY, KB, 128), BF16),
            pltpu.VMEM((NXC, KB, 128), BF16),
            pltpu.VMEM((QN, 128), BF16),
            pltpu.VMEM((QN, 128), BF16),
            pltpu.VMEM((QN, 128), BF16),
            pltpu.VMEM((2, KB, 128), BF16),
            pltpu.VMEM((QN, 128), BF16),
            pltpu.VMEM((NXC, 8, 128), F32),
            pltpu.VMEM((NY, 8, 128), F32),
            pltpu.VMEM((NZ, 8, 128), F32),
            pltpu.VMEM((16, 128), F32),
            pltpu.VMEM((16, 128), F32),
            pltpu.VMEM((16, 128), F32),
            pltpu.VMEM((128, 128), F32),
            pltpu.VMEM((NXC, KB, QN), BF16),
            pltpu.VMEM((NXC, KB, QN), F32),
            pltpu.VMEM((NXC, 8, QN), F32),
            pltpu.VMEM((NY, 8, QN), F32),
            pltpu.VMEM((128, QN), F32),
            pltpu.VMEM((128, QN), F32),
            pltpu.VMEM((2, NZ, QN), F32),
            pltpu.VMEM((NY, HD, KB), F32),
            pltpu.VMEM((NY, HD, KB), F32),
            pltpu.VMEM((NY, HD, KB), BF16),
            pltpu.VMEM((NY, HD, KB), BF16),
            pltpu.VMEM((NXC, KB, 128), BF16),
            pltpu.VMEM((NXC, KB, 128), BF16),
            pltpu.VMEM((NXC, TILE_TYPES, 128), F32),
            pltpu.VMEM((NY, TILE_TYPES, 128), F32),
            pltpu.VMEM((2 * NZ, TILE_TYPES, 128), F32),
            pltpu.VMEM((NZ, ROWS, 128), BF16),
            pltpu.VMEM((NZ, ROWS, 128), BF16),
            pltpu.VMEM((NZ, ROWS, 128), BF16),
            pltpu.VMEM((NZ, ROWS, 128), BF16),
            pltpu.SemaphoreType.DMA((16,)),
            pltpu.SemaphoreType.DMA((N_SEMS,)),
        ],
        compiler_params=pltpu.CompilerParams(
            collective_id=0, has_side_effects=True, vmem_limit_bytes=56 * 1024 * 1024
        ),
        cost_estimate=pl.CostEstimate(
            flops=12 * QN * NXC * KB * 128, bytes_accessed=600_000, transcendentals=QN * NXC * KB
        ),
    )(node_query, node_key, node_value, out_grad, tile_mask, tile_type, edge_table, edge_proj)


def solution(mesh):
    split = P("grid", "head")
    return jax.shard_map(
        per_device,
        mesh=mesh,
        in_specs=(split, split, split, split, P("grid", None, None), P("grid", None, None), P(), P()),
        out_specs=(split, split, split, split, P(), P()),
        check_vma=False,
    )
```

time: 771 us -> 74.1 us (0.10)
  starting transfers between devices: 274 us -> 0 us
  waiting for transfers between devices: 229 us -> 0 us
  blocking collectives: 114 us -> 0 us
  matrix products: 83.7 us -> 0 us
  Pallas kernels: 0 us -> 65.5 us
  local copies, waits for them, and re-layouts: 40.4 us -> 6.61 us
  other arithmetic: 22.8 us -> 0 us
    ppermute x88 -> x0, starting transfers between devices: 274 us -> none  [partner(): return lax.ppermute(block, axis, route)]
    ppermute x88 -> x0, waiting for transfers between devices: 229 us -> none  [partner(): return lax.ppermute(block, axis, route)]
    psum x1 -> x0, blocking collectives: 114 us -> none  [per_device(): type_grad = lax.psum(placed, ('grid', 'head'))]
    dot_general x61 -> x0, matrix products: 83.7 us -> none  [the longest x16 21.2 us: score_block(): jnp.dot(query_head, key_head.T, preferred_element_type=jnp.float32)]
    pallas_call x0 -> x1, Pallas kernels: none -> 65.5 us  [per_device(): pl.pallas_call(kernel, out_shape=(jax.ShapeDtypeStruct(half, BF16), jax.S...]
    broadcast_in_dim x34 -> x0, local copies, waits for them, and re-layouts: 18.7 us -> none  [the longest x8 12.8 us: per_device(): jnp.repeat(jnp.repeat(fwd_mask + rev_mask > 0, TILE, axis=0), TILE, axis=1)]
    select_n x58 -> x0, other arithmetic: 10.7 us -> none  [the longest x34 5.98 us: select_by(): jnp.where(condition, first_leaf, second_leaf)]
  transfers between devices with their start and end apart: 88 -> 0, of which waited for: 38 -> 0; matrix products, arithmetic and copies ran while one was open for 3% -> 0% of each run, Pallas kernels for 0% -> 0%
where the time goes in v1:
time: 74.1 us; the launch traced here: 72.7 us
  Pallas kernels  65.5 us (88%)
  local copies, waits for them, and re-layouts  6.61 us (9%)
    pallas_call x1, Pallas kernels, per_device(): pl.pallas_call(kernel, out_shape=(jax.ShapeDtypeStruct(half, BF16), jax.S...  65.5 us
    unnamed x16, local copies, waits for them, and re-layouts  5.07 us
    pallas_call x1, local copies, waits for them, and re-layouts, per_device(): pl.pallas_call(kernel, out_shape=(jax.ShapeDtypeStruct(half, BF16), jax.S...  1.54 us

profile of v1, /device:TPU:1, one launch (start us, length us, event | category | flops | bytes accessed | tf_op | source)
XLA Modules:
  0.0 72.7 jit_solution(16894150893761805717)
XLA Ops:
  0.6 1.4 %copy.14.proj_ref = f32[128,16]{1,0:T(8,128)} copy(f32[128,16]{0,1:T(8,128)} %param.15) | data formatting | bytes 16384 | tf_op args[7]
  2.1 65.5 %shard_map.127 = (bf16[32,512]{1,0:T(8,128)(2,1)}, f32[32,512]{1,0:T(8,128)}, f32[32,512]{1,0:T(8,128)}, f32[32,512]{1,0:T(8,128)}, f32[16,128]{1,0:T(8,128)}, /*index=5*/f32[128,16]{1,0:T(8,128)}) custom-call(bf16[32,512]{1,0:T(8,128)(2,1)} %q_ref.1, bf16[32,512]{1,0:T(8,128)(2,1)} %k_ref.1, bf16[32,512]{1,0:T(8,128)(2,1)} %v_ref.1, ...), custom_call_target="tpu_custom_call" | custom-call | flops 3221225472 | bytes 600000 | tf_op jit(solution)/shard_map/pallas_call | solution.py:354
  67.5 0.0 copy-start.3
  67.5 0.0 copy-start.2
  67.5 1.5 %copy.15 = f32[128,16]{0,1:T(8,128)} copy(f32[128,16]{1,0:T(8,128)} %get-tuple-element.11) | data formatting | bytes 16384 | tf_op jit(solution)/shard_map/pallas_call | solution.py:354
  69.1 0.0 copy-done.3
  69.1 0.6 copy.21
  69.7 0.0 copy-done.2
  69.7 0.0 copy-start.1
  69.7 0.6 copy.22
  70.3 0.2 copy-done.1
  70.6 0.0 copy-start
  70.6 0.6 copy.23
  71.2 0.2 copy-done
  71.4 0.0 copy-start.4
  71.4 0.6 copy.24
  72.1 0.1 copy-done.4
  72.1 0.6 copy.25
Async XLA Ops:
  67.5 1.6 %copy-start.3 = (bf16[32,512]{1,0:T(8,128)(2,1)S(1)}, bf16[32,512]{1,0:T(8,128)(2,1)}, u32[]{:S(2)}) copy-start(bf16[32,512]{1,0:T(8,128)(2,1)} %get-tuple-element.18) | copy-start | bytes 98308
  67.5 2.2 %copy-start.2 = (f32[32,512]{1,0:T(8,128)S(1)}, f32[32,512]{1,0:T(8,128)}, u32[]{:S(2)}) copy-start(f32[32,512]{1,0:T(8,128)} %get-tuple-element.19) | copy-start | bytes 196612
  69.7 0.9 %copy-start.1 = (f32[32,512]{1,0:T(8,128)S(1)}, f32[32,512]{1,0:T(8,128)}, u32[]{:S(2)}) copy-start(f32[32,512]{1,0:T(8,128)} %get-tuple-element.20) | copy-start | bytes 196612
  70.6 0.9 %copy-start = (f32[32,512]{1,0:T(8,128)S(1)}, f32[32,512]{1,0:T(8,128)}, u32[]{:S(2)}) copy-start(f32[32,512]{1,0:T(8,128)} %get-tuple-element.21) | copy-start | bytes 196612
  71.4 0.7 copy-start.4

commit v2 on v1

v2 whole, which is shorter than its diff:
```python
import jax
import jax.numpy as jnp
from jax import lax
from jax.experimental import pallas as pl
from jax.experimental.pallas import tpu as pltpu
from jax.sharding import PartitionSpec as P

F32 = jnp.float32
BF16 = jnp.bfloat16
MESH = pl.DeviceIdType.MESH

NZ, NY, NX, NC = 8, 4, 4, 2
NXC = NX * NC
ROWS = 32
HALF = ROWS // 2
HD = 64
TYPES = 16
QN = NY * NZ * ROWS
KB = NZ * ROWS
MASKED = -1e30
QCHUNK = 256
CHUNKS = [slice(c * QCHUNK, (c + 1) * QCHUNK) for c in range(QN // QCHUNK)]
FAR_FIRST = (2, 3, 1, 0)

(G_AQ, G_AK, G_MZ, G_MX, G_MY, G_QD, G_ST, G_O, G_DQ, G_RS, G_TX, G_TY, G_TZ, G_X0, G_X1, G_X2, G_KV, G_PR) = range(18)
S_KV = 18
S_PR = S_KV + NXC
N_SEMS = S_PR + NX


def dot_nt(a, b):
    return lax.dot_general(a, b, (((1,), (1,)), ((), ())), preferred_element_type=F32)


def dot_nn(a, b):
    return lax.dot_general(a, b, (((1,), (0,)), ((), ())), preferred_element_type=F32)


def split3(x):
    hi = x.astype(BF16)
    rest = x - hi.astype(F32)
    mid = rest.astype(BF16)
    low = (rest - mid.astype(F32)).astype(BF16)
    return hi, mid, low


def iota(shape, dim):
    return lax.broadcasted_iota(jnp.int32, shape, dim)


def one_hot(condition):
    return jnp.where(condition, 1.0, 0.0).astype(BF16)


def fold(row):
    return jnp.concatenate([row[:, i * 128 : (i + 1) * 128] for i in range(QN // 128)], axis=0)


def unfold(square):
    return jnp.concatenate([square[i : i + 1, :] for i in range(QN // 128)], axis=1)


def half_rows(full):
    full = full.reshape(NZ, ROWS, HD)
    return jnp.concatenate([full[:, 0:HALF], full[:, HALF:ROWS]], axis=2).astype(BF16)


def kernel(
    q_ref, k_ref, v_ref, do_ref, mask_ref, type_ref, table_ref, projt_ref,
    x0_ref, x1_ref, x2_ref, tg_ref,
    stq, stk, qd, kvb, q0, d0, qt, dt, konehot, expand,
    mz, mx, my, fsel, gsel, square,
    sbuf, dbuf, exps, dprob, tops, stat, packed, out_t, dqt, tsum,
    osend, orecv, dsend, drecv, psend, precv, rsend, rrecv,
    tx, ty, tz, x0s, x0r, x1s, x1r, x2s, x2r,
    send, recv,
):
    g = lax.axis_index("grid")
    zh = lax.axis_index("head")
    core = g % 2
    x = (g // 2) % 4
    y = (g // 8) % 4
    z = g // 32
    xc = g % 8
    zf = zh * NZ + z

    def dev(z_, y_, xc_, zh_):
        return ((z_ * NY + y_) * NXC + xc_, zh_)

    def put(src, dst, group, where, slot=None):
        pltpu.make_async_remote_copy(
            src_ref=src, dst_ref=dst, send_sem=send.at[group],
            recv_sem=recv.at[group if slot is None else slot],
            device_id=where, device_id_type=MESH,
        ).start()

    def await_bytes(ref, sem):
        pltpu.make_async_copy(ref, ref, sem).wait()

    z_peers = [(z + d) % NZ for d in range(1, NZ)]
    y_peers = [(y + d) % NY for d in range(1, NY)]
    x_peers = [(x + d) % NX for d in range(1, NX)]
    xc_peers = [(xc + d) % NXC for d in range(1, NXC)]
    zf_peers = [(zf + d) % (2 * NZ) for d in range(1, 2 * NZ)]

    barrier = pltpu.get_barrier_semaphore()
    for p in zf_peers:
        pl.semaphore_signal(barrier, inc=1, device_id=dev(p % NZ, y, xc, p // NZ), device_id_type=MESH)
    for p in y_peers:
        pl.semaphore_signal(barrier, inc=1, device_id=dev(z, p, xc, zh), device_id_type=MESH)
    for p in xc_peers:
        pl.semaphore_signal(barrier, inc=1, device_id=dev(z, y, p, zh), device_id_type=MESH)

    lanes = iota((1, 128), 1)
    code = jnp.zeros((1, 128), jnp.int32)
    for a in range(4):
        for b in range(4):
            value = mask_ref[0, a, b] * (type_ref[0, a, b] + 1)
            code = jnp.where(lanes == z * 16 + (a * 4 + b), value, code)
    mz[z] = code.astype(F32)

    for h in range(NZ):
        cols = slice(h * HD, (h + 1) * HD)
        scaled = (q_ref[:, cols].astype(F32) * 0.125).astype(BF16)
        stq[h] = jnp.concatenate([scaled, do_ref[:, cols]], axis=1)
        stk[h] = jnp.concatenate([k_ref[:, cols], v_ref[:, cols]], axis=1)

    pl.semaphore_wait(barrier, len(xc_peers) + len(y_peers) + len(zf_peers))

    own_rows = pl.ds(pl.multiple_of(z * ROWS, ROWS), ROWS)
    for p in z_peers:
        put(mz.at[z], mz.at[z], G_MZ, dev(p, y, xc, zh))
    for p in z_peers:
        put(stk.at[p], kvb.at[xc, own_rows], G_AK, dev(p, y, xc, zh))
        put(stq.at[p], qd.at[y, own_rows], G_AQ, dev(p, y, xc, zh))
    kvb[xc, own_rows] = stk[z]
    qd[y, own_rows] = stq[z]

    kn = iota((KB, 128), 1)
    kt = iota((KB, 128), 0) // ROWS
    for par in range(2):
        konehot[par] = one_hot((kn < 48) & (kn % 16 == 2 * kt + par))
    qi = iota((QN, 128), 0)
    q_tile = 8 * ((qi % KB) // ROWS) + 2 * (qi // KB) + x // 2
    expand[...] = one_hot(iota((QN, 128), 1) == q_tile)
    stat[...] = jnp.where(iota((8, QN), 0) == 0, -3e38, 0.0)
    out_t[...] = jnp.zeros_like(out_t)
    dqt[...] = jnp.zeros_like(dqt)
    tsum[...] = jnp.zeros_like(tsum)
    square[...] = jnp.zeros((128, 128), F32)

    await_bytes(mz.at[pl.ds(0, 7)], recv.at[G_MZ])
    total = mz[0]
    for i in range(1, NZ):
        total = total + mz[i]
    mx[xc] = total
    for p in xc_peers:
        put(mx.at[xc], mx.at[xc], G_MX, dev(z, y, p, zh))

    await_bytes(mx.at[pl.ds(0, 7)], recv.at[G_MX])
    my[y] = jnp.concatenate([mx[i] for i in range(NXC)], axis=0)
    for p in y_peers:
        put(my.at[y], my.at[y], G_MY, dev(z, p, xc, zh))

    await_bytes(stk.at[pl.ds(0, 7)], recv.at[G_AK])
    for d in (1, 2, 6, 3, 7, 4, 5):
        p = ((x + d // 2) % NX) * 2 + (core + d) % 2
        put(kvb.at[xc], kvb.at[xc], G_KV, dev(z, y, p, zh), slot=S_KV + xc)
    await_bytes(stq.at[pl.ds(0, 7)], recv.at[G_AQ])
    for p in y_peers:
        put(qd.at[y], qd.at[y], G_QD, dev(z, p, xc, zh))

    await_bytes(my.at[pl.ds(0, 3)], recv.at[G_MY])
    codes = my[...].reshape(NY * NXC, 128).astype(BF16)
    pick_b, pick_a = iota((256, 128), 0) // 64, iota((256, 128), 0) % 64
    picked = dot_nt(one_hot(iota((256, 128), 1) == (pick_a // 8) * 16 + (pick_a % 4) * 4 + pick_b), codes)
    same_half = (iota((256, 32), 0) // 4) % 2 == iota((256, 32), 1) // 16
    picked = jnp.where(same_half, picked, 0.0).astype(BF16)
    fcode = jnp.zeros((64, 128), F32)
    for b in range(4):
        spread = one_hot(iota((32, 128), 1) == 4 * (iota((32, 128), 0) % 16) + b)
        fcode = fcode + dot_nn(picked[b * 64 : (b + 1) * 64], spread)
    square[0:64] = fcode
    gcode = jnp.transpose(square[...])[0:64]
    own_proj = projt_ref[pl.ds(zf, 1), :]
    type_bias = jnp.sum(table_ref[...] * own_proj, axis=1, keepdims=True)
    type_bias = jnp.broadcast_to(type_bias, (TYPES, 128))
    bias = jnp.zeros((64, 128), F32)
    for t in range(TYPES):
        here = type_bias[t : t + 1, :]
        bias = bias + jnp.where(fcode == t + 1.0, here, 0.0) + jnp.where(gcode == t + 1.0, here, 0.0)
    bias = jnp.where(fcode + gcode > 0.0, bias, MASKED)
    sel_n = iota((128, 128), 1)
    sel_b = sel_n % 16
    column = iota((128, 128), 0) == 8 * (sel_b // 2) + 2 * y + sel_b % 2
    columns = jnp.zeros((64, 128), F32)
    for part, piece in enumerate(split3(bias)):
        columns = columns + dot_nn(piece, one_hot(column & (sel_n // 16 == part)))
    columns = columns.astype(BF16)
    qt[128:256, :] = jnp.transpose(dot_nn(expand[:, 0:64], columns)).astype(BF16)
    kr = iota((16, 64), 0)
    pick_rows = one_hot(iota((16, 64), 1) == 8 * (kr % 8) + 2 * y + kr // 8)
    fsel[...] = dot_nn(pick_rows, gcode.astype(BF16))
    gsel[...] = dot_nn(pick_rows, fcode.astype(BF16))

    await_bytes(qd.at[pl.ds(0, 3)], recv.at[G_QD])
    low_lanes = jnp.where(lanes < HD, 1.0, 0.0)
    both = qd[...].reshape(QN, 128).astype(F32)
    q_only = both * low_lanes
    d_only = both * (1.0 - low_lanes)
    q0[...] = q_only.astype(BF16)
    d0[...] = d_only.astype(BF16)
    qt[0:128, :] = jnp.transpose(q_only).astype(BF16)
    dt[...] = jnp.transpose(d_only).astype(BF16)

    def block_at(i, c):
        return ((x + i) % NX) * 2 + (core + c) % 2

    order = [block_at(i, c) for i in reversed(FAR_FIRST) for c in range(NC)]

    def products(s):
        j = order[s]
        if s > 0:
            await_bytes(kvb.at[j], recv.at[S_KV + j])
        kv = kvb[j]
        sbuf[s % 2] = dot_nn(jnp.concatenate([kv, konehot[j // 4]], axis=1), qt[...])
        dbuf[s % 2] = dot_nn(kv, dt[...])

    def forward(s):
        j = order[s]
        kvt = jnp.transpose(kvb[j])
        for cs in CHUNKS:
            scores = sbuf[s % 2, :, cs]
            dp = dbuf[s % 2, :, cs]
            dprob[j, :, cs] = dp
            old = stat[0:1, cs]
            top = jnp.maximum(old, jnp.max(scores, axis=0, keepdims=True))
            e = jnp.exp(scores - top)
            shrink = jnp.exp(old - top)
            eb = e.astype(BF16)
            exps[j, :, cs] = eb
            stat[0:1, cs] = top
            stat[1:2, cs] = stat[1:2, cs] * shrink + jnp.sum(e, axis=0, keepdims=True)
            stat[2:3, cs] = stat[2:3, cs] * shrink + jnp.sum(e * dp, axis=0, keepdims=True)
            tops[j, 0:1, cs] = top
            out_t[:, cs] = out_t[:, cs] * shrink + dot_nn(kvt, eb)

    products(0)
    for s in range(NXC):
        if s + 1 < NXC:
            products(s + 1)
        forward(s)

    for i in range(3):
        packed[y, i] = fold(stat[i : i + 1, :])
    for p in y_peers:
        put(packed.at[y], packed.at[y], G_ST, dev(z, p, xc, zh))
    await_bytes(packed.at[pl.ds(0, 3)], recv.at[G_ST])
    top = packed[0, 0]
    for i in range(1, NY):
        top = jnp.maximum(top, packed[i, 0])
    weight_sum = jnp.zeros((8, 128), F32)
    delta = jnp.zeros((8, 128), F32)
    for i in range(NY):
        scale = jnp.exp(packed[i, 0] - top)
        weight_sum = weight_sum + packed[i, 1] * scale
        delta = delta + packed[i, 2] * scale
    delta = unfold(delta / weight_sum)
    logsum = unfold(top + jnp.log(weight_sum))
    own_scale = unfold(jnp.exp(packed[y, 0] - top) / weight_sum)
    for p in range(NY):
        cs = slice(p * KB, (p + 1) * KB)
        osend[p] = out_t[HD : 2 * HD, cs] * own_scale[:, cs]
    orecv[y] = osend[y]
    for p in y_peers:
        put(osend.at[p], orecv.at[y], G_O, dev(z, p, xc, zh))

    def backward(j):
        kv = kvb[j]
        kvt = jnp.transpose(kv)
        dkv = jnp.zeros((KB, 128), F32)
        for cs in CHUNKS:
            sigma = jnp.exp(tops[j, 0:1, cs] - logsum[:, cs])
            p = exps[j, :, cs].astype(F32) * sigma
            ds = p * (dprob[j, :, cs] - delta[:, cs])
            pb = p.astype(BF16)
            dsb = ds.astype(BF16)
            dkv = dkv + dot_nn(pb, d0[cs]) + dot_nn(dsb, q0[cs])
            dqt[:, cs] = dqt[:, cs] + dot_nn(kvt, dsb)
            tsum[j // 4, :, cs] = tsum[j // 4, :, cs] + jnp.sum(ds.reshape(NZ, ROWS, QCHUNK), axis=1)
        return dkv

    other = (core + 1) % 2

    def add_partner(n, dkv):
        await_bytes(precv.at[n], recv.at[S_PR + n])
        return dkv + precv[n].astype(F32)

    waiting = None
    for n, i in enumerate(FAR_FIRST):
        psend[n] = backward(block_at(i, 1)).astype(BF16)
        put(psend.at[n], precv.at[n], G_PR, dev(z, y, x * 2 + other, zh), slot=S_PR + n)
        if waiting is not None:
            rsend[n - 1] = add_partner(n - 1, waiting).astype(BF16)
            put(rsend.at[n - 1], rrecv.at[x], G_RS, dev(z, y, block_at(FAR_FIRST[n - 1], 0), zh))
        if n == 3:
            await_bytes(orecv.at[pl.ds(0, 3)], recv.at[G_O])
            att = orecv[0] + orecv[1] + orecv[2] + orecv[3]
            x0s[...] = half_rows(jnp.transpose(att))
            for p in z_peers:
                put(x0s.at[p], x0r.at[z], G_X0, dev(p, y, xc, zh))
            x0r[z] = x0s[z]
        waiting = backward(block_at(i, 0))

    for p in range(NY):
        dsend[p] = (dqt[0:HD, p * KB : (p + 1) * KB] * 0.125).astype(BF16)
    drecv[y] = dsend[y]
    for p in y_peers:
        put(dsend.at[p], drecv.at[y], G_DQ, dev(z, p, xc, zh))

    sums = jnp.zeros((16, 128), F32)
    for piece in split3(tsum[...].reshape(16, QN)):
        sums = sums + dot_nn(piece, expand[...])
    for t in range(TYPES):
        hits = jnp.where(fsel[...] == t + 1.0, sums, 0.0) + jnp.where(gsel[...] == t + 1.0, sums, 0.0)
        square[t : t + 1, :] = jnp.sum(hits, axis=0, keepdims=True)
    square[TYPES:64, :] = jnp.zeros((64 - TYPES, 128), F32)
    tx[xc] = jnp.sum(jnp.transpose(square[...]), axis=0, keepdims=True)
    for p in xc_peers:
        put(tx.at[xc], tx.at[xc], G_TX, dev(z, y, p, zh))

    own = add_partner(3, waiting)
    await_bytes(rrecv.at[pl.ds(0, 3)], recv.at[G_RS])
    for i in (1, 2, 3):
        own = own + rrecv[(x + i) % NX].astype(F32)
    x2s[...] = own.astype(BF16).reshape(NZ, ROWS, 128)
    for p in z_peers:
        put(x2s.at[p], x2r.at[z], G_X2, dev(p, y, xc, zh))
    x2r[z] = x2s[z]

    await_bytes(tx.at[pl.ds(0, 7)], recv.at[G_TX])
    total = tx[0]
    for i in range(1, NXC):
        total = total + tx[i]
    ty[y] = total
    for p in y_peers:
        put(ty.at[y], ty.at[y], G_TY, dev(z, p, xc, zh))

    await_bytes(drecv.at[pl.ds(0, 3)], recv.at[G_DQ])
    dq = drecv[0].astype(F32) + drecv[1].astype(F32) + drecv[2].astype(F32) + drecv[3].astype(F32)
    x1s[...] = half_rows(jnp.transpose(dq))
    for p in z_peers:
        put(x1s.at[p], x1r.at[z], G_X1, dev(p, y, xc, zh))
    x1r[z] = x1s[z]

    await_bytes(ty.at[pl.ds(0, 3)], recv.at[G_TY])
    tz[zf] = ty[0] + ty[1] + ty[2] + ty[3]
    for p in zf_peers:
        put(tz.at[zf], tz.at[zf], G_TZ, dev(p % NZ, y, xc, p // NZ))

    for ref, group in (
        (stk.at[pl.ds(0, 7)], G_AK), (stq.at[pl.ds(0, 7)], G_AQ), (mz.at[pl.ds(0, 7)], G_MZ),
        (mx.at[pl.ds(0, 7)], G_MX), (my.at[pl.ds(0, 3)], G_MY), (qd.at[pl.ds(0, 3)], G_QD),
        (kvb.at[pl.ds(0, 7)], G_KV), (packed.at[pl.ds(0, 3)], G_ST), (osend.at[pl.ds(0, 3)], G_O),
        (psend.at[pl.ds(0, 4)], G_PR), (dsend.at[pl.ds(0, 3)], G_DQ), (rsend.at[pl.ds(0, 3)], G_RS),
        (tx.at[pl.ds(0, 7)], G_TX), (ty.at[pl.ds(0, 3)], G_TY), (x0s.at[pl.ds(0, 7)], G_X0),
        (x2s.at[pl.ds(0, 7)], G_X2), (x1s.at[pl.ds(0, 7)], G_X1), (tz.at[pl.ds(0, 15)], G_TZ),
    ):
        await_bytes(ref, send.at[group])

    await_bytes(x0r.at[pl.ds(0, 7)], recv.at[G_X0])
    x0_ref[...] = x0r[...]
    await_bytes(x2r.at[pl.ds(0, 7)], recv.at[G_X2])
    x2_ref[...] = x2r[...]
    await_bytes(x1r.at[pl.ds(0, 7)], recv.at[G_X1])
    x1_ref[...] = x1r[...]
    await_bytes(tz.at[pl.ds(0, 15)], recv.at[G_TZ])
    tg_ref[...] = jnp.concatenate([tz[h] for h in range(2 * NZ)], axis=0)


def lay_out(
    x0_ref, x1_ref, x2_ref, tg_ref, table_ref, projt_ref,
    att_ref, dq_ref, dk_ref, dv_ref, dtable_ref, dprojt_ref, square,
):
    low, high = slice(0, HD), slice(HD, 2 * HD)
    for h in range(NZ):
        cols = slice(h * HD, (h + 1) * HD)
        att_ref[0:HALF, cols] = x0_ref[h][:, low]
        att_ref[HALF:ROWS, cols] = x0_ref[h][:, high]
        dq_ref[0:HALF, cols] = x1_ref[h][:, low].astype(F32)
        dq_ref[HALF:ROWS, cols] = x1_ref[h][:, high].astype(F32)
        dk_ref[:, cols] = x2_ref[h][:, low].astype(F32)
        dv_ref[:, cols] = x2_ref[h][:, high].astype(F32)
    tg = tg_ref[...]
    square[...] = jnp.zeros((128, 128), F32)
    square[0:16] = tg
    tg_t = jnp.transpose(square[...])
    dtable = jnp.zeros((TYPES, 128), F32)
    dprojt = jnp.zeros((2 * NZ, 128), F32)
    for i in range(16):
        dtable = dtable + tg_t[0:16, i : i + 1] * projt_ref[i : i + 1, :]
        dprojt = dprojt + tg[:, i : i + 1] * table_ref[i : i + 1, :]
    dtable_ref[...] = dtable
    dprojt_ref[...] = dprojt


def per_device(node_query, node_key, node_value, out_grad, tile_mask, tile_type, edge_table, edge_proj):
    vmem = pl.BlockSpec(memory_space=pltpu.VMEM)
    smem = pl.BlockSpec(memory_space=pltpu.SMEM)
    half = (ROWS, NZ * HD)
    proj_t = edge_proj.T
    spread = pl.pallas_call(
        kernel,
        out_shape=(
            jax.ShapeDtypeStruct((NZ, HALF, 128), BF16),
            jax.ShapeDtypeStruct((NZ, HALF, 128), BF16),
            jax.ShapeDtypeStruct((NZ, ROWS, 128), BF16),
            jax.ShapeDtypeStruct((2 * NZ, 128), F32),
        ),
        in_specs=[vmem] * 4 + [smem] * 2 + [vmem] * 2,
        out_specs=(vmem,) * 4,
        scratch_shapes=[
            pltpu.VMEM((NZ, ROWS, 128), BF16),
            pltpu.VMEM((NZ, ROWS, 128), BF16),
            pltpu.VMEM((NY, KB, 128), BF16),
            pltpu.VMEM((NXC, KB, 128), BF16),
            pltpu.VMEM((QN, 128), BF16),
            pltpu.VMEM((QN, 128), BF16),
            pltpu.VMEM((256, QN), BF16),
            pltpu.VMEM((128, QN), BF16),
            pltpu.VMEM((2, KB, 128), BF16),
            pltpu.VMEM((QN, 128), BF16),
            pltpu.VMEM((NZ, 1, 128), F32),
            pltpu.VMEM((NXC, 1, 128), F32),
            pltpu.VMEM((NY, NXC, 128), F32),
            pltpu.VMEM((16, 128), F32),
            pltpu.VMEM((16, 128), F32),
            pltpu.VMEM((128, 128), F32),
            pltpu.VMEM((2, KB, QN), F32),
            pltpu.VMEM((2, KB, QN), F32),
            pltpu.VMEM((NXC, KB, QN), BF16),
            pltpu.VMEM((NXC, KB, QN), F32),
            pltpu.VMEM((NXC, 8, QN), F32),
            pltpu.VMEM((8, QN), F32),
            pltpu.VMEM((NY, 3, 8, 128), F32),
            pltpu.VMEM((128, QN), F32),
            pltpu.VMEM((128, QN), F32),
            pltpu.VMEM((2, NZ, QN), F32),
            pltpu.VMEM((NY, HD, KB), F32),
            pltpu.VMEM((NY, HD, KB), F32),
            pltpu.VMEM((NY, HD, KB), BF16),
            pltpu.VMEM((NY, HD, KB), BF16),
            pltpu.VMEM((NX, KB, 128), BF16),
            pltpu.VMEM((NX, KB, 128), BF16),
            pltpu.VMEM((NX, KB, 128), BF16),
            pltpu.VMEM((NX, KB, 128), BF16),
            pltpu.VMEM((NXC, 1, 128), F32),
            pltpu.VMEM((NY, 1, 128), F32),
            pltpu.VMEM((2 * NZ, 1, 128), F32),
            pltpu.VMEM((NZ, HALF, 128), BF16),
            pltpu.VMEM((NZ, HALF, 128), BF16),
            pltpu.VMEM((NZ, HALF, 128), BF16),
            pltpu.VMEM((NZ, HALF, 128), BF16),
            pltpu.VMEM((NZ, ROWS, 128), BF16),
            pltpu.VMEM((NZ, ROWS, 128), BF16),
            pltpu.SemaphoreType.DMA((18,)),
            pltpu.SemaphoreType.DMA((N_SEMS,)),
        ],
        compiler_params=pltpu.CompilerParams(
            collective_id=0, has_side_effects=True, vmem_limit_bytes=56 * 1024 * 1024
        ),
        cost_estimate=pl.CostEstimate(
            flops=12 * QN * NXC * KB * 128, bytes_accessed=600_000, transcendentals=QN * NXC * KB
        ),
    )(node_query, node_key, node_value, out_grad, tile_mask, tile_type, edge_table, proj_t)
    att, dq, dk, dv, dtable, dprojt = pl.pallas_call(
        lay_out,
        out_shape=(
            jax.ShapeDtypeStruct(half, BF16),
            jax.ShapeDtypeStruct(half, F32),
            jax.ShapeDtypeStruct(half, F32),
            jax.ShapeDtypeStruct(half, F32),
            jax.ShapeDtypeStruct((TYPES, 128), F32),
            jax.ShapeDtypeStruct((2 * NZ, 128), F32),
        ),
        in_specs=[vmem] * 6,
        out_specs=(vmem,) * 6,
        scratch_shapes=[pltpu.VMEM((128, 128), F32)],
    )(*spread, edge_table, proj_t)
    return att, dq, dk, dv, dtable, dprojt.T


def solution(mesh):
    split = P("grid", "head")
    return jax.shard_map(
        per_device,
        mesh=mesh,
        in_specs=(split, split, split, split, P("grid", None, None), P("grid", None, None), P(), P()),
        out_specs=(split, split, split, split, P(), P()),
        check_vma=False,
    )
```

time: 74.1 us -> 64.1 us (0.87); the launches traced: 72.7 us -> 63.9 us
  local copies, waits for them, and re-layouts: 6.61 us -> 0 us
  Pallas kernels: 65.5 us -> 63.2 us
    unnamed x16 -> x0, local copies, waits for them, and re-layouts: 5.07 us -> none
    pallas_call x1 -> x2, Pallas kernels: 65.5 us -> 63.2 us  [the longest x1 61.5 us: per_device(): pl.pallas_call(kernel, out_shape=(jax.ShapeDtypeStruct((NZ, HALF, 128), B...]
    pallas_call x1 -> x0, local copies, waits for them, and re-layouts: 1.54 us -> none  [per_device(): pl.pallas_call(kernel, out_shape=(jax.ShapeDtypeStruct(half, BF16), jax.S...]
where the time goes in v2:
time: 64.1 us; the launch traced here: 63.9 us
  Pallas kernels  63.2 us (99%)
    pallas_call x1, Pallas kernels, per_device(): pl.pallas_call(kernel, out_shape=(jax.ShapeDtypeStruct((NZ, HALF, 128), B...  61.5 us
    pallas_call x1, Pallas kernels, per_device(): pl.pallas_call(lay_out, out_shape=(jax.ShapeDtypeStruct(half, BF16), jax....  1.75 us

profile of v2, /device:TPU:1, one launch (start us, length us, event | category | flops | bytes accessed | tf_op | source)
XLA Modules:
  0.0 63.9 jit_solution(16516022045059046861)
XLA Ops:
  0.6 61.5 %shard_map.127 = (bf16[8,16,128]{2,1,0:T(8,128)(2,1)}, bf16[8,16,128]{2,1,0:T(8,128)(2,1)}, bf16[8,32,128]{2,1,0:T(8,128)(2,1)}, f32[16,128]{1,0:T(8,128)}) custom-call(bf16[32,512]{1,0:T(8,128)(2,1)} %q_ref.1, bf16[32,512]{1,0:T(8,128)(2,1)} %k_ref.1, bf16[32,512]{1,0:T(8,128)(2,1)} %v_ref.1, bf16[32,512]{1,0:T(8,128)(2,1)} %do_ref.1, s32[1,4,4]{2,1,0:T(4,128)} %mask_ref.1, ...), custom_call_target="tpu_custom_call" | custom-call | flops 3221225472 | bytes 600000 | tf_op jit(solution)/shard_map/pallas_call | solution.py:412
  62.1 1.8 %shard_map.128 = (bf16[32,512]{1,0:T(8,128)(2,1)}, f32[32,512]{1,0:T(8,128)}, f32[32,512]{1,0:T(8,128)}, f32[32,512]{1,0:T(8,128)}, f32[16,128]{1,0:T(8,128)}, /*index=5*/f32[16,128]{1,0:T(8,128)}) custom-call(bf16[8,16,128]{2,1,0:T(8,128)(2,1)} %get-tuple-element.16.x0_ref, bf16[8,16,128]{2,1,0:T(8,128)(2,1)} %get-tuple-element.17.x1_ref, ...), custom_call_target="tpu_custom_call" | custom-call | tf_op jit(solution)/shard_map/pallas_call | solution.py:476

commit v3 on v2

--- a/solution.py
+++ b/solution.py
@@ -11,6 +11,7 @@
 
 NZ, NY, NX, NC = 8, 4, 4, 2
 NXC = NX * NC
+PLANE = NY * NXC
 ROWS = 32
 HALF = ROWS // 2
 HD = 64
@@ -22,8 +23,8 @@
 CHUNKS = [slice(c * QCHUNK, (c + 1) * QCHUNK) for c in range(QN // QCHUNK)]
 FAR_FIRST = (2, 3, 1, 0)
 
-(G_AQ, G_AK, G_MZ, G_MX, G_MY, G_QD, G_ST, G_O, G_DQ, G_RS, G_TX, G_TY, G_TZ, G_X0, G_X1, G_X2, G_KV, G_PR) = range(18)
-S_KV = 18
+(G_AQ, G_AK, G_MZ, G_MX, G_QD, G_ST, G_O, G_DQ, G_RS, G_TX, G_TZ, G_X0, G_X1, G_X2, G_KV, G_PR) = range(16)
+S_KV = 16
 S_PR = S_KV + NXC
 N_SEMS = S_PR + NX
 
@@ -69,10 +70,10 @@
     q_ref, k_ref, v_ref, do_ref, mask_ref, type_ref, table_ref, projt_ref,
     x0_ref, x1_ref, x2_ref, tg_ref,
     stq, stk, qd, kvb, q0, d0, qt, dt, konehot, expand,
-    mz, mx, my, fsel, gsel, square,
+    mz, mx, fsel, gsel, square,
     sbuf, dbuf, exps, dprob, tops, stat, packed, out_t, dqt, tsum,
     osend, orecv, dsend, drecv, psend, precv, rsend, rrecv,
-    tx, ty, tz, x0s, x0r, x1s, x1r, x2s, x2r,
+    tx, tz, x0s, x0r, x1s, x1r, x2s, x2r,
     send, recv,
 ):
     g = lax.axis_index("grid")
@@ -82,6 +83,7 @@
     y = (g // 8) % 4
     z = g // 32
     xc = g % 8
+    n_plane = g % PLANE
     zf = zh * NZ + z
 
     def dev(z_, y_, xc_, zh_):
@@ -97,19 +99,37 @@
     def await_bytes(ref, sem):
         pltpu.make_async_copy(ref, ref, sem).wait()
 
-    z_peers = [(z + d) % NZ for d in range(1, NZ)]
-    y_peers = [(y + d) % NY for d in range(1, NY)]
-    x_peers = [(x + d) % NX for d in range(1, NX)]
-    xc_peers = [(xc + d) % NXC for d in range(1, NXC)]
-    zf_peers = [(zf + d) % (2 * NZ) for d in range(1, 2 * NZ)]
+    def in_plane(d):
+        return (z * PLANE + (n_plane + d) % PLANE, zh)
+
+    def to_plane(slots, group):
+        def step(d, carry):
+            put(slots.at[n_plane], slots.at[n_plane], group, in_plane(d))
+            return carry
+
+        lax.fori_loop(1, PLANE, step, 0)
+
+    def each(count, me):
+        def run(act):
+            def step(d, carry):
+                act((me + d) % count)
+                return carry
+
+            lax.fori_loop(1, count, step, 0)
+
+        return run
 
     barrier = pltpu.get_barrier_semaphore()
-    for p in zf_peers:
+
+    @each(2 * NZ, zf)
+    def _(p):
         pl.semaphore_signal(barrier, inc=1, device_id=dev(p % NZ, y, xc, p // NZ), device_id_type=MESH)
-    for p in y_peers:
-        pl.semaphore_signal(barrier, inc=1, device_id=dev(z, p, xc, zh), device_id_type=MESH)
-    for p in xc_peers:
-        pl.semaphore_signal(barrier, inc=1, device_id=dev(z, y, p, zh), device_id_type=MESH)
+
+    def greet(d, carry):
+        pl.semaphore_signal(barrier, inc=1, device_id=in_plane(d), device_id_type=MESH)
+        return carry
+
+    lax.fori_loop(1, PLANE, greet, 0)
 
     lanes = iota((1, 128), 1)
     code = jnp.zeros((1, 128), jnp.int32)
@@ -125,14 +145,19 @@
         stq[h] = jnp.concatenate([scaled, do_ref[:, cols]], axis=1)
         stk[h] = jnp.concatenate([k_ref[:, cols], v_ref[:, cols]], axis=1)
 
-    pl.semaphore_wait(barrier, len(xc_peers) + len(y_peers) + len(zf_peers))
+    pl.semaphore_wait(barrier, PLANE - 1 + 2 * NZ - 1)
 
     own_rows = pl.ds(pl.multiple_of(z * ROWS, ROWS), ROWS)
-    for p in z_peers:
+
+    @each(NZ, z)
+    def _(p):
         put(mz.at[z], mz.at[z], G_MZ, dev(p, y, xc, zh))
-    for p in z_peers:
+
+    @each(NZ, z)
+    def _(p):
         put(stk.at[p], kvb.at[xc, own_rows], G_AK, dev(p, y, xc, zh))
         put(stq.at[p], qd.at[y, own_rows], G_AQ, dev(p, y, xc, zh))
+
     kvb[xc, own_rows] = stk[z]
     qd[y, own_rows] = stq[z]
 
@@ -153,25 +178,24 @@
     total = mz[0]
     for i in range(1, NZ):
         total = total + mz[i]
-    mx[xc] = total
-    for p in xc_peers:
-        put(mx.at[xc], mx.at[xc], G_MX, dev(z, y, p, zh))
-
-    await_bytes(mx.at[pl.ds(0, 7)], recv.at[G_MX])
-    my[y] = jnp.concatenate([mx[i] for i in range(NXC)], axis=0)
-    for p in y_peers:
-        put(my.at[y], my.at[y], G_MY, dev(z, p, xc, zh))
+    mx[n_plane] = total
+    to_plane(mx, G_MX)
 
     await_bytes(stk.at[pl.ds(0, 7)], recv.at[G_AK])
-    for d in (1, 2, 6, 3, 7, 4, 5):
-        p = ((x + d // 2) % NX) * 2 + (core + d) % 2
+
+    @each(NXC, core)
+    def _(d):
+        p = ((x + d // 2) % NX) * 2 + d % 2
         put(kvb.at[xc], kvb.at[xc], G_KV, dev(z, y, p, zh), slot=S_KV + xc)
+
     await_bytes(stq.at[pl.ds(0, 7)], recv.at[G_AQ])
-    for p in y_peers:
+
+    @each(NY, y)
+    def _(p):
         put(qd.at[y], qd.at[y], G_QD, dev(z, p, xc, zh))
 
-    await_bytes(my.at[pl.ds(0, 3)], recv.at[G_MY])
-    codes = my[...].reshape(NY * NXC, 128).astype(BF16)
+    await_bytes(mx.at[pl.ds(0, PLANE - 1)], recv.at[G_MX])
+    codes = jnp.concatenate([mx[i] for i in range(PLANE)], axis=0).astype(BF16)
     pick_b, pick_a = iota((256, 128), 0) // 64, iota((256, 128), 0) % 64
     picked = dot_nt(one_hot(iota((256, 128), 1) == (pick_a // 8) * 16 + (pick_a % 4) * 4 + pick_b), codes)
     same_half = (iota((256, 32), 0) // 4) % 2 == iota((256, 32), 1) // 16
@@ -253,8 +277,11 @@
 
     for i in range(3):
         packed[y, i] = fold(stat[i : i + 1, :])
-    for p in y_peers:
+
+    @each(NY, y)
+    def _(p):
         put(packed.at[y], packed.at[y], G_ST, dev(z, p, xc, zh))
+
     await_bytes(packed.at[pl.ds(0, 3)], recv.at[G_ST])
     top = packed[0, 0]
     for i in range(1, NY):
@@ -270,10 +297,8 @@
     own_scale = unfold(jnp.exp(packed[y, 0] - top) / weight_sum)
     for p in range(NY):
         cs = slice(p * KB, (p + 1) * KB)
-        osend[p] = out_t[HD : 2 * HD, cs] * own_scale[:, cs]
+        osend[p] = (out_t[HD : 2 * HD, cs] * own_scale[:, cs]).astype(BF16)
     orecv[y] = osend[y]
-    for p in y_peers:
-        put(osend.at[p], orecv.at[y], G_O, dev(z, p, xc, zh))
 
     def backward(j):
         kv = kvb[j]
@@ -296,26 +321,32 @@
         await_bytes(precv.at[n], recv.at[S_PR + n])
         return dkv + precv[n].astype(F32)
 
-    waiting = None
+    def pass_on(n, dkv):
+        rsend[n] = add_partner(n, dkv).astype(BF16)
+        put(rsend.at[n], rrecv.at[x], G_RS, dev(z, y, block_at(FAR_FIRST[n], 0), zh))
+
+    partials = []
     for n, i in enumerate(FAR_FIRST):
         psend[n] = backward(block_at(i, 1)).astype(BF16)
         put(psend.at[n], precv.at[n], G_PR, dev(z, y, x * 2 + other, zh), slot=S_PR + n)
-        if waiting is not None:
-            rsend[n - 1] = add_partner(n - 1, waiting).astype(BF16)
-            put(rsend.at[n - 1], rrecv.at[x], G_RS, dev(z, y, block_at(FAR_FIRST[n - 1], 0), zh))
-        if n == 3:
-            await_bytes(orecv.at[pl.ds(0, 3)], recv.at[G_O])
-            att = orecv[0] + orecv[1] + orecv[2] + orecv[3]
-            x0s[...] = half_rows(jnp.transpose(att))
-            for p in z_peers:
-                put(x0s.at[p], x0r.at[z], G_X0, dev(p, y, xc, zh))
-            x0r[z] = x0s[z]
-        waiting = backward(block_at(i, 0))
+        if n == 0:
+
+            @each(NY, y)
+            def _(p):
+                put(osend.at[p], orecv.at[y], G_O, dev(z, p, xc, zh))
+
+        partials.append(backward(block_at(i, 0)))
+        if n == 2:
+            pass_on(0, partials[0])
+    pass_on(1, partials[1])
+    pass_on(2, partials[2])
 
     for p in range(NY):
         dsend[p] = (dqt[0:HD, p * KB : (p + 1) * KB] * 0.125).astype(BF16)
     drecv[y] = dsend[y]
-    for p in y_peers:
+
+    @each(NY, y)
+    def _(p):
         put(dsend.at[p], drecv.at[y], G_DQ, dev(z, p, xc, zh))
 
     sums = jnp.zeros((16, 128), F32)
@@ -325,45 +356,59 @@
         hits = jnp.where(fsel[...] == t + 1.0, sums, 0.0) + jnp.where(gsel[...] == t + 1.0, sums, 0.0)
         square[t : t + 1, :] = jnp.sum(hits, axis=0, keepdims=True)
     square[TYPES:64, :] = jnp.zeros((64 - TYPES, 128), F32)
-    tx[xc] = jnp.sum(jnp.transpose(square[...]), axis=0, keepdims=True)
-    for p in xc_peers:
-        put(tx.at[xc], tx.at[xc], G_TX, dev(z, y, p, zh))
-
-    own = add_partner(3, waiting)
+    tx[n_plane] = jnp.sum(jnp.transpose(square[...]), axis=0, keepdims=True)
+    to_plane(tx, G_TX)
+
+    await_bytes(orecv.at[pl.ds(0, 3)], recv.at[G_O])
+    att = orecv[0].astype(F32)
+    for p in range(1, NY):
+        att = att + orecv[p].astype(F32)
+    x0s[...] = half_rows(jnp.transpose(att))
+
+    @each(NZ, z)
+    def _(p):
+        put(x0s.at[p], x0r.at[z], G_X0, dev(p, y, xc, zh))
+
+    x0r[z] = x0s[z]
+
+    own = add_partner(NX - 1, partials[3])
     await_bytes(rrecv.at[pl.ds(0, 3)], recv.at[G_RS])
     for i in (1, 2, 3):
         own = own + rrecv[(x + i) % NX].astype(F32)
     x2s[...] = own.astype(BF16).reshape(NZ, ROWS, 128)
-    for p in z_peers:
+
+    @each(NZ, z)
+    def _(p):
         put(x2s.at[p], x2r.at[z], G_X2, dev(p, y, xc, zh))
+
     x2r[z] = x2s[z]
-
-    await_bytes(tx.at[pl.ds(0, 7)], recv.at[G_TX])
-    total = tx[0]
-    for i in range(1, NXC):
-        total = total + tx[i]
-    ty[y] = total
-    for p in y_peers:
-        put(ty.at[y], ty.at[y], G_TY, dev(z, p, xc, zh))
 
     await_bytes(drecv.at[pl.ds(0, 3)], recv.at[G_DQ])
     dq = drecv[0].astype(F32) + drecv[1].astype(F32) + drecv[2].astype(F32) + drecv[3].astype(F32)
     x1s[...] = half_rows(jnp.transpose(dq))
-    for p in z_peers:
+
+    @each(NZ, z)
+    def _(p):
         put(x1s.at[p], x1r.at[z], G_X1, dev(p, y, xc, zh))
+
     x1r[z] = x1s[z]
 
-    await_bytes(ty.at[pl.ds(0, 3)], recv.at[G_TY])
-    tz[zf] = ty[0] + ty[1] + ty[2] + ty[3]
-    for p in zf_peers:
+    await_bytes(tx.at[pl.ds(0, PLANE - 1)], recv.at[G_TX])
+    total = tx[0]
+    for i in range(1, PLANE):
+        total = total + tx[i]
+    tz[zf] = total
+
+    @each(2 * NZ, zf)
+    def _(p):
         put(tz.at[zf], tz.at[zf], G_TZ, dev(p % NZ, y, xc, p // NZ))
 
     for ref, group in (
         (stk.at[pl.ds(0, 7)], G_AK), (stq.at[pl.ds(0, 7)], G_AQ), (mz.at[pl.ds(0, 7)], G_MZ),
-        (mx.at[pl.ds(0, 7)], G_MX), (my.at[pl.ds(0, 3)], G_MY), (qd.at[pl.ds(0, 3)], G_QD),
+        (mx.at[pl.ds(0, PLANE - 1)], G_MX), (qd.at[pl.ds(0, 3)], G_QD),
         (kvb.at[pl.ds(0, 7)], G_KV), (packed.at[pl.ds(0, 3)], G_ST), (osend.at[pl.ds(0, 3)], G_O),
         (psend.at[pl.ds(0, 4)], G_PR), (dsend.at[pl.ds(0, 3)], G_DQ), (rsend.at[pl.ds(0, 3)], G_RS),
-        (tx.at[pl.ds(0, 7)], G_TX), (ty.at[pl.ds(0, 3)], G_TY), (x0s.at[pl.ds(0, 7)], G_X0),
+        (tx.at[pl.ds(0, PLANE - 1)], G_TX), (x0s.at[pl.ds(0, 7)], G_X0),
         (x2s.at[pl.ds(0, 7)], G_X2), (x1s.at[pl.ds(0, 7)], G_X1), (tz.at[pl.ds(0, 15)], G_TZ),
     ):
         await_bytes(ref, send.at[group])
@@ -431,8 +476,7 @@
             pltpu.VMEM((2, KB, 128), BF16),
             pltpu.VMEM((QN, 128), BF16),
             pltpu.VMEM((NZ, 1, 128), F32),
-            pltpu.VMEM((NXC, 1, 128), F32),
-            pltpu.VMEM((NY, NXC, 128), F32),
+            pltpu.VMEM((PLANE, 1, 128), F32),
             pltpu.VMEM((16, 128), F32),
             pltpu.VMEM((16, 128), F32),
             pltpu.VMEM((128, 128), F32),
@@ -446,16 +490,15 @@
             pltpu.VMEM((128, QN), F32),
             pltpu.VMEM((128, QN), F32),
             pltpu.VMEM((2, NZ, QN), F32),
-            pltpu.VMEM((NY, HD, KB), F32),
-            pltpu.VMEM((NY, HD, KB), F32),
+            pltpu.VMEM((NY, HD, KB), BF16),
+            pltpu.VMEM((NY, HD, KB), BF16),
             pltpu.VMEM((NY, HD, KB), BF16),
             pltpu.VMEM((NY, HD, KB), BF16),
             pltpu.VMEM((NX, KB, 128), BF16),
             pltpu.VMEM((NX, KB, 128), BF16),
             pltpu.VMEM((NX, KB, 128), BF16),
             pltpu.VMEM((NX, KB, 128), BF16),
-            pltpu.VMEM((NXC, 1, 128), F32),
-            pltpu.VMEM((NY, 1, 128), F32),
+            pltpu.VMEM((PLANE, 1, 128), F32),
             pltpu.VMEM((2 * NZ, 1, 128), F32),
             pltpu.VMEM((NZ, HALF, 128), BF16),
             pltpu.VMEM((NZ, HALF, 128), BF16),
@@ -463,7 +506,7 @@
             pltpu.VMEM((NZ, HALF, 128), BF16),
             pltpu.VMEM((NZ, ROWS, 128), BF16),
             pltpu.VMEM((NZ, ROWS, 128), BF16),
-            pltpu.SemaphoreType.DMA((18,)),
+            pltpu.SemaphoreType.DMA((16,)),
             pltpu.SemaphoreType.DMA((N_SEMS,)),
         ],
         compiler_params=pltpu.CompilerParams(

time: 64.1 us -> 61.6 us (0.961)
  Pallas kernels: 63.2 us -> 60.7 us
    pallas_call x1, Pallas kernels: 61.5 us -> 59 us  [per_device(): pl.pallas_call(kernel, out_shape=(jax.ShapeDtypeStruct((NZ, HALF, 128), B...]
where the time goes in v3:
time: 61.6 us; the launch traced here: 61.4 us
  Pallas kernels  60.7 us (99%)
  between operations  0.64 us (1%)
    pallas_call x1, Pallas kernels, per_device(): pl.pallas_call(kernel, out_shape=(jax.ShapeDtypeStruct((NZ, HALF, 128), B...  59 us
    pallas_call x1, Pallas kernels, per_device(): pl.pallas_call(lay_out, out_shape=(jax.ShapeDtypeStruct(half, BF16), jax....  1.75 us

profile of v3, /device:TPU:1, one launch (start us, length us, event | category | flops | bytes accessed | tf_op | source)
XLA Modules:
  0.0 61.4 jit_solution(14708257612256303803)
XLA Ops:
  0.6 59.0 %shard_map.127 = (bf16[8,16,128]{2,1,0:T(8,128)(2,1)}, bf16[8,16,128]{2,1,0:T(8,128)(2,1)}, bf16[8,32,128]{2,1,0:T(8,128)(2,1)}, f32[16,128]{1,0:T(8,128)}) custom-call(bf16[32,512]{1,0:T(8,128)(2,1)} %q_ref.1, bf16[32,512]{1,0:T(8,128)(2,1)} %k_ref.1, bf16[32,512]{1,0:T(8,128)(2,1)} %v_ref.1, bf16[32,512]{1,0:T(8,128)(2,1)} %do_ref.1, s32[1,4,4]{2,1,0:T(4,128)} %mask_ref.1, ...), custom_call_target="tpu_custom_call" | custom-call | flops 3221225472 | bytes 600000 | tf_op jit(solution)/shard_map/pallas_call | solution.py:457
  59.6 1.8 %shard_map.128 = (bf16[32,512]{1,0:T(8,128)(2,1)}, f32[32,512]{1,0:T(8,128)}, f32[32,512]{1,0:T(8,128)}, f32[32,512]{1,0:T(8,128)}, f32[16,128]{1,0:T(8,128)}, /*index=5*/f32[16,128]{1,0:T(8,128)}) custom-call(bf16[8,16,128]{2,1,0:T(8,128)(2,1)} %get-tuple-element.16.x0_ref, bf16[8,16,128]{2,1,0:T(8,128)(2,1)} %get-tuple-element.17.x1_ref, ...), custom_call_target="tpu_custom_call" | custom-call | tf_op jit(solution)/shard_map/pallas_call | solution.py:519

commit v4 on v3

--- a/solution.py
+++ b/solution.py
@@ -341,14 +341,6 @@
     pass_on(1, partials[1])
     pass_on(2, partials[2])
 
-    for p in range(NY):
-        dsend[p] = (dqt[0:HD, p * KB : (p + 1) * KB] * 0.125).astype(BF16)
-    drecv[y] = dsend[y]
-
-    @each(NY, y)
-    def _(p):
-        put(dsend.at[p], drecv.at[y], G_DQ, dev(z, p, xc, zh))
-
     sums = jnp.zeros((16, 128), F32)
     for piece in split3(tsum[...].reshape(16, QN)):
         sums = sums + dot_nn(piece, expand[...])
@@ -358,6 +350,14 @@
     square[TYPES:64, :] = jnp.zeros((64 - TYPES, 128), F32)
     tx[n_plane] = jnp.sum(jnp.transpose(square[...]), axis=0, keepdims=True)
     to_plane(tx, G_TX)
+
+    for p in range(NY):
+        dsend[p] = (dqt[0:HD, p * KB : (p + 1) * KB] * 0.125).astype(BF16)
+    drecv[y] = dsend[y]
+
+    @each(NY, y)
+    def _(p):
+        put(dsend.at[p], drecv.at[y], G_DQ, dev(z, p, xc, zh))
 
     await_bytes(orecv.at[pl.ds(0, 3)], recv.at[G_O])
     att = orecv[0].astype(F32)

time: 61.6 us -> 61.6 us (level)
  no operation moved by 1% of the time
where the time goes in v4:
time: 61.6 us; the launch traced here: 61.4 us
  Pallas kernels  60.7 us (99%)
  between operations  0.64 us (1%)
    pallas_call x1, Pallas kernels, per_device(): pl.pallas_call(kernel, out_shape=(jax.ShapeDtypeStruct((NZ, HALF, 128), B...  59 us
    pallas_call x1, Pallas kernels, per_device(): pl.pallas_call(lay_out, out_shape=(jax.ShapeDtypeStruct(half, BF16), jax....  1.75 us

profile of v4, /device:TPU:1, one launch (start us, length us, event | category | flops | bytes accessed | tf_op | source)
XLA Modules:
  0.0 61.4 jit_solution(17060233367472100031)
XLA Ops:
  0.6 59.0 %shard_map.127 = (bf16[8,16,128]{2,1,0:T(8,128)(2,1)}, bf16[8,16,128]{2,1,0:T(8,128)(2,1)}, bf16[8,32,128]{2,1,0:T(8,128)(2,1)}, f32[16,128]{1,0:T(8,128)}) custom-call(bf16[32,512]{1,0:T(8,128)(2,1)} %q_ref.1, bf16[32,512]{1,0:T(8,128)(2,1)} %k_ref.1, bf16[32,512]{1,0:T(8,128)(2,1)} %v_ref.1, bf16[32,512]{1,0:T(8,128)(2,1)} %do_ref.1, s32[1,4,4]{2,1,0:T(4,128)} %mask_ref.1, ...), custom_call_target="tpu_custom_call" | custom-call | flops 3221225472 | bytes 600000 | tf_op jit(solution)/shard_map/pallas_call | solution.py:457
  59.6 1.8 %shard_map.128 = (bf16[32,512]{1,0:T(8,128)(2,1)}, f32[32,512]{1,0:T(8,128)}, f32[32,512]{1,0:T(8,128)}, f32[32,512]{1,0:T(8,128)}, f32[16,128]{1,0:T(8,128)}, /*index=5*/f32[16,128]{1,0:T(8,128)}) custom-call(bf16[8,16,128]{2,1,0:T(8,128)(2,1)} %get-tuple-element.16.x0_ref, bf16[8,16,128]{2,1,0:T(8,128)(2,1)} %get-tuple-element.17.x1_ref, ...), custom_call_target="tpu_custom_call" | custom-call | tf_op jit(solution)/shard_map/pallas_call | solution.py:519
